TPU v7x, 256 devices: a whole 4x4x8 slice. The times are simulated.
256 devices in a mesh: row: 8 (over z), col: 8 (over x_hi, y), samp: 4 (over x_lo, core).
Axes of the slice: x: 4 (x_hi: 2, x_lo: 2; x = x_hi * 2 + x_lo), y: 4, z: 8, core: 2. Of those that a mesh axis runs over, the one named last changes fastest.
Arguments:
- pair: bfloat16 [768, 768, 128], P('row', 'col'), may hold values from -6 to 6
- crop_mask: int32 [768], replicated, may hold values 0 or 1
- w_agate: bfloat16 [128, 128], replicated, may hold values from -0.5 to 0.5
- w_aval: bfloat16 [128, 128], replicated, may hold values from -0.5 to 0.5
- w_bgate: bfloat16 [128, 128], replicated, may hold values from -0.5 to 0.5
- w_bval: bfloat16 [128, 128], replicated, may hold values from -0.5 to 0.5
- w_outgate: bfloat16 [128, 128], replicated, may hold values from -0.5 to 0.5
- w_outproj: bfloat16 [128, 128], replicated, may hold values from -0.5 to 0.5
- ln_pair: float32 [128], replicated, may hold values from 0.1 to 1.9
- w_trans_gate: bfloat16 [128, 512], replicated, may hold values from -0.5 to 0.5
- w_trans_up: bfloat16 [128, 512], replicated, may hold values from -0.5 to 0.5
- w_trans_down: bfloat16 [512, 128], replicated, may hold values from -0.25 to 0.25
- ln_bias: float32 [128], replicated, may hold values from 0.1 to 1.9
- w_pairbias: bfloat16 [128, 16], replicated, may hold values from -0.5 to 0.5
- tokens: bfloat16 [16, 768, 768], P('samp', 'row', 'col'), may hold values from -6 to 6
- ln_token: float32 [768], replicated, may hold values from 0.1 to 1.9
- w_query: bfloat16 [768, 768], P(None, 'col'), may hold values from -1 to 1
- w_key: bfloat16 [768, 768], P(None, 'col'), may hold values from -1 to 1
- w_value: bfloat16 [768, 768], P(None, 'col'), may hold values from -0.21875 to 0.21875
- w_gate: bfloat16 [768, 768], P(None, 'col'), may hold values from -0.21875 to 0.21875
- w_output: bfloat16 [768, 768], P('col'), may hold values from -0.21875 to 0.21875
- cotangent: bfloat16 [16, 768, 768], P('samp', 'row', 'col'), may hold values from -6 to 6
Outputs:
- pair_out: bfloat16 [768, 768, 128], P('row', 'col')
- tokens_out: bfloat16 [16, 768, 768], P('samp', 'row', 'col')
- pair_grad: float32 [768, 768, 128], P('row', 'col')
All inputs are finite; a program needn't handle non-finite values.
Results may differ from a plain program's by a relative error of at most 0.015.
Values may be sent and summed in bfloat16 or wider, within the bound.
A program may use at most 128 MiB of HBM per device.

v0:
```python
import math

import jax
import jax.numpy as jnp
from jax import lax
from jax.sharding import PartitionSpec as P


def normalize(values):
    center = values - jnp.mean(values, axis=-1, keepdims=True)
    return center * lax.rsqrt(jnp.mean(center * center, axis=-1, keepdims=True) + 1e-05)


def pair_transition(pair_rows, w_trans_gate, w_trans_up, w_trans_down):
    trans_in = normalize(pair_rows.astype(jnp.float32)).astype(jnp.bfloat16)
    gate_part = jax.nn.silu(jnp.dot(trans_in, w_trans_gate, preferred_element_type=jnp.float32))
    hidden = (gate_part * jnp.dot(trans_in, w_trans_up, preferred_element_type=jnp.float32)).astype(
        jnp.bfloat16
    )
    return (
        pair_rows.astype(jnp.float32)
        + jnp.dot(hidden, w_trans_down, preferred_element_type=jnp.float32)
    ).astype(jnp.bfloat16)


def transition_blocks(pair_rows, w_trans_gate, w_trans_up, w_trans_down):
    row_total, col_total, width = pair_rows.shape
    step_rows = math.gcd(row_total, 12)

    def one_block(block_rows):
        return pair_transition(block_rows, w_trans_gate, w_trans_up, w_trans_down)

    stacked = pair_rows.reshape(row_total // step_rows, step_rows, col_total, width)
    return lax.map(one_block, stacked).reshape(row_total, col_total, width)


def per_device(
    pair,
    crop_mask,
    w_agate,
    w_aval,
    w_bgate,
    w_bval,
    w_outgate,
    w_outproj,
    ln_pair,
    w_trans_gate,
    w_trans_up,
    w_trans_down,
    ln_bias,
    w_pairbias,
    tokens,
    ln_token,
    w_query,
    w_key,
    w_value,
    w_gate,
    w_output,
    cotangent,
):
    row_total, col_total, width = pair.shape
    row_index = lax.axis_index("row")
    col_index = lax.axis_index("col")
    samp_index = lax.axis_index("samp")
    samp_count = lax.axis_size("samp")
    keep = crop_mask.astype(jnp.float32)
    keep_rows = lax.dynamic_slice_in_dim(keep, row_index * row_total, row_total)
    keep_cols = lax.dynamic_slice_in_dim(keep, col_index * col_total, col_total)
    pair_keep = (keep_rows[:, None] * keep_cols[None, :])[:, :, None]
    floats = pair.astype(jnp.float32)
    normed = (normalize(floats) * ln_pair).astype(jnp.bfloat16)
    quarter = width // samp_count

    def channel_slice(weight):
        return lax.dynamic_slice_in_dim(weight, samp_index * quarter, quarter, 1)

    left = (
        jax.nn.sigmoid(jnp.dot(normed, channel_slice(w_agate), preferred_element_type=jnp.float32))
        * jnp.dot(normed, channel_slice(w_aval), preferred_element_type=jnp.float32)
        * pair_keep
    ).astype(jnp.bfloat16)
    right = (
        jax.nn.sigmoid(jnp.dot(normed, channel_slice(w_bgate), preferred_element_type=jnp.float32))
        * jnp.dot(normed, channel_slice(w_bval), preferred_element_type=jnp.float32)
        * pair_keep
    ).astype(jnp.bfloat16)
    partial_sums = jnp.einsum(
        "ikc,jkc->ijc",
        left,
        lax.all_gather(right, "row", axis=0, tiled=True),
        preferred_element_type=jnp.float32,
    )
    triangle = lax.psum_scatter(partial_sums, "col", scatter_dimension=1, tiled=True).astype(
        jnp.bfloat16
    )
    all_channels = lax.all_gather(triangle, "samp", axis=2, tiled=True)
    tri_norm = normalize(all_channels.astype(jnp.float32)).astype(jnp.bfloat16)
    out_gate = jax.nn.sigmoid(jnp.dot(normed, w_outgate, preferred_element_type=jnp.float32))
    updated = (
        floats + out_gate * jnp.dot(tri_norm, w_outproj, preferred_element_type=jnp.float32)
    ).astype(jnp.bfloat16)
    pair_out = transition_blocks(updated, w_trans_gate, w_trans_up, w_trans_down)
    final = pair_out.astype(jnp.float32)
    center = final - jnp.mean(final, axis=-1, keepdims=True)
    inv_scale = lax.rsqrt(jnp.mean(center * center, axis=-1, keepdims=True) + 1e-05)
    unit = center * inv_scale
    bias_in = (unit * ln_bias).astype(jnp.bfloat16)
    bias_heads = jnp.einsum(
        "ijc,ch->hij", bias_in, w_pairbias, preferred_element_type=jnp.float32
    ).astype(jnp.bfloat16)
    head_bias = lax.all_to_all(bias_heads, "col", split_axis=0, concat_axis=2, tiled=True).astype(
        jnp.float32
    )
    local_heads = head_bias.shape[0]
    token_full, grad_full = (
        lax.all_gather(tokens, "col", axis=2, tiled=True),
        lax.all_gather(cotangent, "col", axis=2, tiled=True),
    )
    samples, token_rows, model_width = token_full.shape
    token_norm = (normalize(token_full.astype(jnp.float32)) * ln_token).astype(jnp.bfloat16)
    query = jnp.dot(token_norm, w_query, preferred_element_type=jnp.float32).astype(jnp.bfloat16)
    keyed = jnp.dot(token_norm, w_key, preferred_element_type=jnp.float32).astype(jnp.bfloat16)
    value = jnp.dot(token_norm, w_value, preferred_element_type=jnp.float32).astype(jnp.bfloat16)
    gate_val = jax.nn.sigmoid(jnp.dot(token_norm, w_gate, preferred_element_type=jnp.float32))
    all_keys, all_values = (
        lax.all_gather(keyed, "row", axis=1, tiled=True),
        lax.all_gather(value, "row", axis=1, tiled=True),
    )
    head_size = query.shape[-1] // local_heads
    key_total = all_keys.shape[1]
    query_heads = query.reshape(samples, token_rows, local_heads, head_size)
    key_heads = all_keys.reshape(samples, key_total, local_heads, head_size)
    value_heads = all_values.reshape(samples, key_total, local_heads, head_size)
    scale = 1.0 / math.sqrt(head_size)
    key_mask = (keep - 1.0) * 10000.0
    scores = (
        jnp.einsum("sihd,sjhd->shij", query_heads, key_heads, preferred_element_type=jnp.float32)
        * scale
        + head_bias[None]
        + key_mask[None, None, None, :]
    )
    shifted = jnp.exp(scores - jnp.max(scores, axis=-1, keepdims=True))
    probs = shifted / jnp.sum(shifted, axis=-1, keepdims=True)
    weights = probs.astype(jnp.bfloat16)
    attended = jnp.einsum(
        "shij,sjhd->sihd", weights, value_heads, preferred_element_type=jnp.float32
    )
    gated = (gate_val * attended.reshape(samples, token_rows, local_heads * head_size)).astype(
        jnp.bfloat16
    )
    projected = jnp.dot(gated, w_output, preferred_element_type=jnp.float32)
    added = lax.psum_scatter(projected, "col", scatter_dimension=2, tiled=True)
    tokens_out = (tokens.astype(jnp.float32) + added).astype(jnp.bfloat16)
    d_gated = jnp.einsum("sie,fe->sif", grad_full, w_output, preferred_element_type=jnp.float32)
    d_att = (
        (d_gated * gate_val)
        .astype(jnp.bfloat16)
        .reshape(samples, token_rows, local_heads, head_size)
    )
    d_probs = jnp.einsum("sihd,sjhd->shij", d_att, value_heads, preferred_element_type=jnp.float32)
    delta = jnp.einsum("sihd,sihd->shi", d_att.astype(jnp.float32), attended)[..., None]
    d_scores = probs * (d_probs - delta)
    local_grad = jnp.sum(d_scores, axis=0)
    summed_grad = lax.psum(local_grad, "samp")
    block_grad = lax.all_to_all(summed_grad, "col", split_axis=2, concat_axis=0, tiled=True)
    back = jnp.einsum(
        "hij,ch->ijc", block_grad, w_pairbias.astype(jnp.float32), precision=lax.Precision.HIGHEST
    )
    scaled = back * ln_bias
    pair_grad = inv_scale * (
        scaled
        - jnp.mean(scaled, axis=-1, keepdims=True)
        - unit * jnp.mean(scaled * unit, axis=-1, keepdims=True)
    )
    return (pair_out, tokens_out, pair_grad)


def solution(mesh):
    placed = (
        P("row", "col", None),
        P(),
        P(),
        P(),
        P(),
        P(),
        P(),
        P(),
        P(),
        P(),
        P(),
        P(),
        P(),
        P(),
        P("samp", "row", "col"),
        P(),
        P(None, "col"),
        P(None, "col"),
        P(None, "col"),
        P(None, "col"),
        P("col", None),
        P("samp", "row", "col"),
    )
    return jax.shard_map(
        per_device,
        mesh=mesh,
        in_specs=placed,
        out_specs=(P("row", "col", None), P("samp", "row", "col"), P("row", "col", None)),
        check_vma=False,
    )
```

profile of v0, /device:TPU:1, one launch (start us, length us, event | category | flops | bytes accessed | tf_op | source)
XLA Modules:
  0.0 645.9 jit_solution(5889538966670231143)
XLA Ops:
  8.1 2.6 convert_reduce_fusion.2
  10.7 3.1 fusion.41
  14.1 2.7 fusion.88
  16.8 5.7 multiply_convert_fusion.4
  22.6 2.7 fusion.85
  25.3 5.5 multiply_convert_fusion.3
  30.8 70.1 %all-gather.3.cloned.1.call-done = bf16[768,96,32]{1,2,0:T(8,128)(2,1)} async-done(((bf16[96,96,32]{1,2,0:T(8,128)(2,1)}), bf16[768,96,32]{1,2,0:T(8,128)(2,1)}) %all-gather.3.cloned.1.call-update) | async-done | bytes 4718608 | tf_op jit(solution)/shard_map/all_gather | solution.py:90
  100.9 13.9 %fusion.47 = f32[96,768,32]{1,0,2:T(8,128)} fusion(bf16[768,96,32]{1,2,0:T(8,128)(2,1)} %all-gather.3.cloned.1.call-done, bf16[96,96,32]{1,2,0:T(8,128)(2,1)S(1)} %multiply_convert_fusion.3), kind=kOutput, calls=%fused_computation.56 | convolution fusion | flops 452984832 | bytes 14745600 | tf_op jit(solution)/shard_map/ikc,jkc->ijc/dot_general | solution.py:87
  114.8 11.7 %copy.118 = f32[96,768,32]{0,2,1:T(8,128)} copy(f32[96,768,32]{1,0,2:T(8,128)} %fusion.47) | data formatting | bytes 18874368
  126.4 13.3 %reshape.183 = f32[768,3072]{1,0:T(8,128)} reshape(f32[768,32,96]{2,1,0:T(8,128)} %bitcast.136) | data formatting | bytes 18874368
  139.9 127.2 %reduce-scatter.7.cloned.1.call-done = f32[96,3072]{1,0:T(8,128)} async-done(((f32[768,3072]{1,0:T(8,128)}), f32[96,3072]{1,0:T(8,128)}) %reduce-scatter.7.cloned.1.call-update) | async-done | bytes 1179664
  267.1 2.0 reshape.184
  269.0 1.7 copy.119
  270.9 33.4 %all_gather.20 = bf16[4,96,768]{1,0,2:T(4,128)(2,1)} all-gather(bf16[4,96,96]{1,0,2:T(4,128)(2,1)S(1)} %copy.95), channel_id=1, replica_groups=mesh['row'=8,'col'=8,'samp'=4] {'col'}, dimensions={2}, use_global_device_ids=true | all-gather | bytes 663552 | tf_op jit(solution)/shard_map/all_gather | solution.py:116
  304.3 1.6 copy.96
  309.7 30.4 %all_gather.23 = bf16[4,96,768]{1,0,2:T(4,128)(2,1)S(1)} all-gather(bf16[4,96,96]{1,0,2:T(4,128)(2,1)S(1)} %copy.103), channel_id=1, replica_groups=mesh['row'=8,'col'=8,'samp'=4] {'col'}, dimensions={2}, use_global_device_ids=true | all-gather | bytes 663552 | tf_op jit(solution)/shard_map/all_gather | solution.py:117
  341.1 23.9 %all_gather.22 = bf16[4,768,96]{2,1,0:T(8,128)(2,1)} all-gather(bf16[4,96,96]{2,1,0:T(8,128)(2,1)S(1)} %convolution_convert_fusion), channel_id=1, replica_groups=mesh['row'=8,'col'=8,'samp'=4] {'row'}, dimensions={1}, use_global_device_ids=true | all-gather | bytes 663552 | tf_op jit(solution)/shard_map/all_gather | solution.py:126
  365.0 22.8 %all_gather.21 = bf16[4,768,96]{2,1,0:T(8,128)(2,1)} all-gather(bf16[4,96,96]{2,1,0:T(8,128)(2,1)S(1)} %convolution_convert_fusion.2), channel_id=1, replica_groups=mesh['row'=8,'col'=8,'samp'=4] {'row'}, dimensions={1}, use_global_device_ids=true | all-gather | bytes 663552 | tf_op jit(solution)/shard_map/all_gather | solution.py:127
  387.8 2.7 convert_reduce_fusion.1
  394.1 5.5 fusion.46
  399.6 56.5 %while.10 = (s32[]{:T(128)}, bf16[8,12,96,128]{3,2,1,0:T(8,128)(2,1)}, bf16[8,12,96,128]{3,2,1,0:T(8,128)(2,1)}, bf16[128,512]{1,0:T(8,128)(2,1)}, bf16[128,512]...) while((s32[]{:T(128)}, bf16[8,12,96,128]{3,2,1,0:T(8,128)(2,1)}, ...), condition=%wide.region_8.9_spmd, body=%wide.region_5.8_spmd.sunk | while | flops 459031680 | bytes 7982221 | solution.py:34
  403.8 2.9 fusion.137
  410.8 2.9 fusion.137
  417.9 2.9 fusion.137
  425.0 2.9 fusion.137
  432.0 2.9 fusion.137
  439.1 2.9 fusion.137
  446.2 2.9 fusion.137
  453.2 2.9 fusion.137
  456.1 2.7 convert_reduce_fusion.3
  458.9 3.2 fusion.45
  462.1 4.0 fusion.60
  467.0 3.7 all-to-all-start
  470.7 1.9 convolution_convert_fusion.1
  472.7 2.2 copy.99
  474.9 1.6 copy.98
  478.1 2.2 copy.97
  482.0 3.7 fusion.115
  485.7 2.4 fusion.77
  491.2 2.5 copy.120
  493.7 2.9 reshape.185
  496.6 59.7 %all-reduce.2.cloned.1.call-done = f32[2,96,768]{2,1,0:T(8,128)} async-done(((f32[2,96,768]{2,1,0:T(8,128)}), f32[2,96,768]{2,1,0:T(8,128)}) %all-reduce.2.cloned.1.call-update) | async-done | bytes 589840 | tf_op jit(solution)/shard_map/psum | solution.py:164
  556.3 2.1 copy.106
  558.4 19.3 %all_to_all.27 = f32[2,96,768]{1,0,2:T(2,128)S(1)} all-to-all(f32[2,96,768]{1,0,2:T(2,128)} %copy.106), channel_id=1, replica_groups=mesh['row'=8,'col'=8,'samp'=4] {'col'}, dimensions={2} | all-to-all | bytes 1179648 | tf_op jit(solution)/shard_map/all_to_all | solution.py:165
  578.9 1.7 copy.108
  580.6 9.4 %multiply_reduce_fusion.1 = (f32[96,96]{1,0:T(8,128)S(1)}, f32[96,96]{1,0:T(8,128)S(1)}, f32[96,96,128]{2,1,0:T(8,128)S(1)}) fusion(f32[128]{0:T(128)S(1)} %copy-done.20, f32[96,96]{1,0:T(8,128)S(1)} %copy-done.10, f32[96,96]{1,0:T(8,128)S(1)} %div.73, bf16[96,96,128]{2,1,0:T(8,128)(2,1)S(1)} %bitcast.139, f32[16,96,96]{2,0,1:T(8,128)S(1)} %bitcast.147, ...), kind=kOutput, calls=%fused_computation.55 | convolution fusion | flops 234731520 | bytes 7819776 | tf_op jit(solution)/shard_map/hij,ch->ijc/dot_general | solution.py:166
  590.1 7.8 %subtract_multiply_fusion = f32[96,96,128]{2,1,0:T(8,128)} fusion(f32[96,96,128]{2,1,0:T(8,128)S(1)} %get-tuple-element.56, f32[96,96]{1,0:T(8,128)S(1)} %broadcast_multiply_fusion.3, f32[96,96]{1,0:T(8,128)S(1)} %broadcast_multiply_fusion.4, f32[128]{0:T(128)S(1)} %copy-done.20, f32[96,96]{1,0:T(8,128)S(1)} %copy-done.10, f32[96,96]{1,0:T(8,128)S(1)} %div.73, ...), kind=kLoop, calls=%fused_computation.51 | loop fusion | flops 9437184 | bytes 11944448 | tf_op jit(solution)/shard_map/mul | solution.py:170
  597.9 39.3 %reduce-scatter.9.cloned.1.call-done = f32[96,384]{1,0:T(8,128)} async-done(((f32[768,384]{1,0:T(8,128)}), f32[96,384]{1,0:T(8,128)}) %reduce-scatter.9.cloned.1.call-update) | async-done | bytes 147472
  (185 shorter events, 52.7 us)
Async XLA Ops:
  7.2 332.9 %copy-start = (bf16[96,768]{1,0:T(8,128)(2,1)S(1)}, bf16[96,768]{1,0:T(8,128)(2,1)}, u32[]{:S(2)}) copy-start(bf16[96,768]{1,0:T(8,128)(2,1)} %param.44) | copy-start | bytes 442372
  7.2 3.5 copy-start.3
  7.2 93.7 %all-gather.3.cloned.1.call-start = ((), (), s32[]{:S(2)}) async-start(), calls=%async_computation.4 | async-start | bytes 7077888 | tf_op jit(solution)/shard_map/all_gather | solution.py:90
  8.1 6.0 copy-start.24
  8.1 6.0 copy-start.32
  14.0 11.2 %copy-start.16 = (f32[96,96]{1,0:T(8,128)}, f32[96,96]{1,0:T(8,128)S(1)}, u32[]{:S(2)}) copy-start(f32[96,96]{1,0:T(8,128)S(1)} %get-tuple-element.57) | copy-start | bytes 110596
  14.1 2.7 copy-start.25
  16.8 5.8 copy-start.26
  22.5 2.8 copy-start.27
  22.5 244.5 %reduce-scatter.7.cloned.1.call-start = ((), (), s32[]{:S(2)}) async-start(), calls=%async_computation.7 | async-start | bytes 10616832
  139.8 131.0 %copy-start.7 = (bf16[4,96,96]{2,1,0:T(8,128)(2,1)S(1)}, bf16[4,96,96]{2,1,0:T(8,128)(2,1)}, u32[]{:S(2)}) copy-start(bf16[4,96,96]{2,1,0:T(8,128)(2,1)} %param.38) | copy-start | bytes 221188
  139.8 248.0 %all-gather.5.cloned.1.call-start = ((), (), s32[]{:S(2)}) async-start(), calls=%async_computation.5 | async-start | bytes 3932160 | tf_op jit(solution)/shard_map/all_gather | solution.py:96
  269.0 37.0 %copy-start.13 = (bf16[4,96,96]{2,1,0:T(8,128)(2,1)S(1)}, bf16[4,96,96]{2,1,0:T(8,128)(2,1)}, u32[]{:S(2)}) copy-start(bf16[4,96,96]{2,1,0:T(8,128)(2,1)} %param.45) | copy-start | bytes 221188
  270.8 35.9 %copy-start.29 = (f32[768]{0:T(1024)S(1)}, f32[768]{0:T(1024)}, u32[]{:S(2)}) copy-start(f32[768]{0:T(1024)} %param.39) | copy-start | bytes 9220
  306.1 3.1 copy-start.21
  309.7 31.5 %copy-start.11 = (f32[4,96,96]{2,1,0:T(8,128)}, f32[4,96,96]{2,1,0:T(8,128)S(1)}, u32[]{:S(2)}) copy-start(f32[4,96,96]{2,1,0:T(8,128)S(1)} %fusion.71) | copy-start | bytes 442372
  387.8 2.8 copy-start.1
  394.1 5.5 copy-start.4
  399.6 4.1 copy-start.22
  399.6 4.2 copy-start.23
  406.6 4.1 copy-start.22
  406.6 4.2 copy-start.23
  413.8 4.1 copy-start.22
  413.8 4.2 copy-start.23
  420.8 4.1 copy-start.22
  420.8 4.2 copy-start.23
  427.9 4.1 copy-start.22
  427.9 4.2 copy-start.23
  434.9 4.1 copy-start.22
  434.9 4.2 copy-start.23
  442.0 4.1 copy-start.22
  442.0 4.2 copy-start.23
  449.1 4.1 copy-start.22
  449.1 4.2 copy-start.23
  456.1 2.8 copy-start.2
  456.1 6.0 copy-start.20
  456.1 6.0 copy-start.30
  462.1 4.0 copy-start.9
  467.0 13.3 %all-to-all-start = ((bf16[16,96,96]{2,1,0:T(8,128)(2,1)}), bf16[16,96,96]{2,1,0:T(8,128)(2,1)S(1)}, u32[]{:S(2)}, u32[]{:S(2)}) async-start(bf16[16,96,96]{2,1,0:T(8,128)(2,1)} %copy.100), calls=%async_computation | async-start | bytes 786432 | tf_op jit(solution)/shard_map/all_to_all | solution.py:111
  470.7 9.7 %copy-start.19 = (s32[768]{0:T(1024)S(1)}, s32[768]{0:T(1024)}, u32[]{:S(2)}) copy-start(s32[768]{0:T(1024)} %param.25) | copy-start | bytes 9220
  470.7 85.6 %all-reduce.2.cloned.1.call-start = ((), (), s32[]{:S(2)}) async-start(), calls=%async_computation.6 | async-start | bytes 1179648 | tf_op jit(solution)/shard_map/psum | solution.py:164
  480.9 4.8 copy-start.14
  482.0 3.7 copy-start.6
  485.7 2.5 copy-start.15
  489.7 147.5 %reduce-scatter.9.cloned.1.call-start = ((), (), s32[]{:S(2)}) async-start(), calls=%async_computation.8 | async-start | bytes 1327104
  558.4 22.2 %copy-start.10 = (f32[96,96]{1,0:T(8,128)S(1)}, f32[96,96]{1,0:T(8,128)}, u32[]{:S(2)}) copy-start(f32[96,96]{1,0:T(8,128)} %copy-done.9) | copy-start | bytes 110596
  558.4 22.2 %copy-start.31 = (bf16[128,16]{0,1:T(8,128)(2,1)S(1)}, bf16[128,16]{0,1:T(8,128)(2,1)}, u32[]{:S(2)}) copy-start(bf16[128,16]{0,1:T(8,128)(2,1)} %param.37) | copy-start | bytes 12292
  590.1 48.4 %copy-start.8 = (bf16[4,96,96]{2,1,0:T(8,128)(2,1)S(1)}, bf16[4,96,96]{2,1,0:T(8,128)(2,1)}, u32[]{:S(2)}) copy-start(bf16[4,96,96]{2,1,0:T(8,128)(2,1)} %param.38) | copy-start | bytes 221188
  (5 other events, 7.9 us)
Sparse Core Ops, SparseCore 0:
  22.6 78.2 all-gather.2
  139.9 127.0 reduce-scatter.6
  270.9 44.4 all-gather.4
  489.8 66.4 all-reduce.1
  560.1 77.1 reduce-scatter.8
where the time goes:
time: 654 us; the launch traced here: 646 us
  waiting for transfers between devices  296 us (45%)
  blocking collectives  130 us (20%)
  matrix products  101 us (15%)
  local copies, waits for them, and re-layouts  52.7 us (8%)
  other arithmetic  47.2 us (7%)
  between operations  14.6 us (2%)
    unnamed x7, waiting for transfers between devices  167 us
    all_gather x1, waiting for transfers between devices, per_device(): lax.all_gather(right, 'row', axis=0, tiled=True)  70.1 us
    psum x1, waiting for transfers between devices, per_device(): summed_grad = lax.psum(local_grad, 'samp')  59.7 us
    unnamed x72, local copies, waits for them, and re-layouts  35.8 us
    all_gather x1, blocking collectives, per_device(): lax.all_gather(tokens, 'col', axis=2, tiled=True)  33.4 us
    all_gather x1, blocking collectives, per_device(): lax.all_gather(cotangent, 'col', axis=2, tiled=True)  30.4 us
    all_gather x1, blocking collectives, per_device(): lax.all_gather(keyed, 'row', axis=1, tiled=True)  23.9 us
    dot_general x8, matrix products, pair_transition(): jnp.dot(hidden, w_trans_down, preferred_element_type=jnp.float32)  23.2 us
  transfers between devices with their start and end apart: 6, of which 4 were waited for; matrix products, arithmetic and copies ran while one was open for 8% of the time, Pallas kernels for 0%

commit v1 on v0

v1 whole, which is shorter than its diff:
```python
import math

import jax
import jax.numpy as jnp
from jax import lax
from jax.experimental import pallas as pl
from jax.experimental.pallas import tpu as pltpu
from jax.sharding import PartitionSpec as P

F32 = jnp.float32
BF16 = jnp.bfloat16
MESH = pl.DeviceIdType.MESH
NR = 8
NC = 8
NS = 4
B = 96
Q = 24
G = 24
CH = 4
RC = 6 * B


def nt(a, b):
    return lax.dot_general(a, b, (((1,), (1,)), ((), ())), preferred_element_type=F32)


def nn(a, b):
    return lax.dot_general(a, b, (((1,), (0,)), ((), ())), preferred_element_type=F32)


def tn(a, b):
    return lax.dot_general(a, b, (((0,), (0,)), ((), ())), preferred_element_type=F32)


def row_means(values, ones):
    high = values.astype(BF16)
    low = (values - high.astype(F32)).astype(BF16)
    return nn(jnp.concatenate([high, low], axis=1), ones)


def centered(values, ones):
    center = values.astype(F32) - nn(values, ones[0:128])
    return center, lax.rsqrt(row_means(center * center, ones) + 1e-05)


def normalize(values, ones):
    center, inv = centered(values, ones)
    return center * inv


def mean_weights():
    return jnp.full((256, 128), 1.0 / 128.0, BF16)


def kernel(
    pair, crop_s, crop_v, w_ag, w_av, w_bg, w_bv, lnp, w_outgate, w_outproj, w_tg, w_tu, w_td,
    lnb, wpbt, tokens, cot, lnt, wq, wk, wv, wg, wo,
    pair_out, tokens_out, bg,
    wt, w_op, xd, cd,
    normed, lf, rf, lm, rslab, part, y_recv, own_sum, x_send, x_recv, tok_slab, cot_slab, q_s, kslab, vslab, gate_s, datt_s,
    tri_send, tri_recv, tri_f, hb_send, hb, bias, acc, pj_send, pj_recv, rs_recv, sg, cg,
    tok_ss, tok_rs, cot_ss, cot_rs, ring_ss, ring_rs, y_ss, y_rs, x_ss, x_rs,
    k_ss, k_rs, v_ss, v_rs, t_ss, t_rs, h_ss, h_rs,
    hg_ss, hg_rs, po_ss, po_rs, pj_ss, pj_rs, g_ss, g_rs, c_ss, c_rs, b_ss, b_rs,
):
    row = lax.axis_index("row")
    col = lax.axis_index("col")
    samp = lax.axis_index("samp")
    xh = col // 4
    yy = col % 4
    xp = (1 - xh) * 4 + yy
    ones = mean_weights()
    right = (row + 1) % NR
    left = (row + NR - 1) % NR

    def copy(src, dst, ss, rs, **where):
        return pltpu.make_async_remote_copy(
            src_ref=src, dst_ref=dst, send_sem=ss, recv_sem=rs, device_id=where, device_id_type=MESH
        )

    barrier = pltpu.get_barrier_semaphore()
    for d in range(1, NC):
        pl.semaphore_signal(barrier, inc=1, device_id={"col": (col + d) % NC}, device_id_type=MESH)
    for d in range(1, NR):
        pl.semaphore_signal(barrier, inc=1, device_id={"row": (row + d) % NR}, device_id_type=MESH)
    for d in range(1, NS):
        pl.semaphore_signal(
            barrier, inc=1, device_id={"samp": (samp + d) % NS}, device_id_type=MESH
        )

    pl.semaphore_wait(barrier, NC + NR + NS - 3)

    def col_all(src_of, slab, ss, rs, d):
        there, here = (col + d) % NC, (col + NC - d) % NC
        return (
            copy(src_of(there), slab.at[col], ss.at[d], rs.at[d], col=there),
            copy(src_of(there), slab.at[here], ss.at[d], rs.at[d], col=there),
        )

    tok_copies = [col_all(lambda _: tokens, tok_slab, tok_ss, tok_rs, d) for d in range(1, NC)]
    cot_copies = [col_all(lambda _: cot, cot_slab, cot_ss, cot_rs, d) for d in range(1, NC)]
    for out, _ in tok_copies + cot_copies:
        out.start()
    tok_slab[col] = tokens[...]
    cot_slab[col] = cot[...]

    for n, w in enumerate((w_ag, w_av, w_bg, w_bv)):
        wt[n] = w[...].astype(F32).T.astype(BF16)
    wp = jnp.concatenate([wt[n, pl.ds(pl.multiple_of(samp * 32, 32), 32), :] for n in range(4)], axis=0)
    tri_f[0:128, :] = w_outproj[...].astype(F32)
    w_op[...] = jnp.concatenate(
        [tri_f[pl.ds(0, 64, stride=2), :], tri_f[pl.ds(1, 64, stride=2), :]], axis=0
    ).astype(BF16)
    keep_cols = jnp.zeros((1, B), F32)
    for b in range(NC):
        here = crop_v[0:1, b * B : b * B + B].astype(F32)
        keep_cols = jnp.where(col == b, here, keep_cols)
    keep_cols = jnp.concatenate([keep_cols, jnp.zeros((1, 32), F32)], axis=1)

    def norm_step(m, carry):
        at = pl.ds(pl.multiple_of(m * 384, 384), 384)
        normed[at, :] = (normalize(pair[at, :], ones) * lnp[...]).astype(BF16)
        return carry

    lax.fori_loop(0, B // 4, norm_step, 0)
    normed[B * B : B * B + 32, :] = jnp.zeros((32, 128), BF16)
    lane = lax.broadcasted_iota(jnp.int32, (8, 128), 1)
    wide = lane < B

    def edge_step(m, carry):
        for e in range(4):
            i = m * 4 + e
            rows = normed[pl.ds(pl.multiple_of(i * B, 32), 128), :]
            o = nt(wp, rows)
            kept = keep_cols * crop_s[row * B + i].astype(F32)
            for first, dest in ((0, lf), (64, rf)):
                edge = jax.nn.sigmoid(o[first : first + 32]) * o[first + 32 : first + 64] * kept
                tail = edge[24:32]
                for q in range(3):
                    packed = jnp.where(
                        wide, edge[8 * q : 8 * q + 8], pltpu.roll(tail, 96 - 32 * q, 1)
                    )
                    dest[pl.ds(i + 8 * B * q, 8, stride=B), :] = packed
        return carry

    lax.fori_loop(0, B // 4, edge_step, 0)

    own = lax.broadcasted_iota(jnp.int32, (B, 128), 1) < B
    for n in range(CH):
        for k in range(6):
            g, q = 2 * n + k // 3, k % 3
            at = pl.ds((q * 8 + g) * B, B)
            rslab[n, row, k * B : k * B + B, :] = rf[at, :].astype(BF16)
            edge = lf[at, :]
            lm[6 * n + k, 0:B, :] = jnp.where(own, edge, 0.0).astype(BF16)
            lm[6 * n + k, B : 2 * B, :] = jnp.where(own, 0.0, edge).astype(BF16)
    for n in range(CH):
        rslab[n, :, RC : RC + 32, :] = jnp.zeros((NR, 32, 128), BF16)

    def token_step(s):
        at = pl.ds(s * B, B)
        x = [tok_slab[b, at, :].astype(F32) for b in range(NC)]
        total = x[0]
        for b in range(1, NC):
            total = total + x[b]
        mean = jnp.sum(total, axis=-1, keepdims=True) * (1.0 / (NC * B))
        x = [v - mean for v in x]
        total = x[0] * x[0]
        for b in range(1, NC):
            total = total + x[b] * x[b]
        scale = lax.rsqrt(jnp.sum(total, axis=-1, keepdims=True) * (1.0 / (NC * B)) + 1e-05)
        for b in range(NC):
            xd[:, b * B : b * B + B] = x[b] * scale
            cd[:, b * B : b * B + B] = cot_slab[b, at, :].astype(F32)
        normal = (xd[...] * lnt[...]).astype(BF16)
        q_s[at, :] = nt(normal, wq[...]).astype(BF16)
        kslab[row, at, :] = nt(normal, wk[...]).astype(BF16)
        vslab[row, at, :] = nt(normal, wv[...]).astype(BF16)
        gate = jax.nn.sigmoid(nt(normal, wg[...]))
        gate_s[at, :] = gate
        d = nt(cd[...].astype(BF16), wo[...])
        datt_s[at, :] = (d * gate).astype(BF16)

    ring = (right, left)
    step_of = (-1, 1)

    def rcopy(n, t, s, inward):
        back = t if inward else t - 1
        block = (row + NR + step_of[s] * back) % NR
        rows = pl.ds(0, RC) if t < 4 else pl.ds(s * (RC // 2), RC // 2)
        at = rslab.at[n, block, rows]
        return copy(at, at, ring_ss.at[n, s, t - 1], ring_rs.at[n, s, t - 1], row=ring[s])

    def product(n, j):
        for gg in range(2):
            tops, tail = [], None
            for q in range(3):
                k = gg * 3 + q
                o = nt(lm[6 * n + k], rslab[n, j, k * B : k * B + 128, :])
                tops.append(o[0:B])
                tail = o[B : 2 * B] if tail is None else tail + o[B : 2 * B]
            for q in range(3):
                k = gg * 3 + q
                packed = jnp.where(own, tops[q], pltpu.roll(tail, 96 - 32 * q, 1))
                part[n, j, k * B : k * B + B, :] = packed.astype(BF16)

    def products(n, back):
        if back in (0, 4):
            product(n, (row + back) % NR)
        else:

            def one(d, carry):
                product(n, (row + NR + (2 * d - 1) * back) % NR)
                return carry

            lax.fori_loop(0, 2, one, 0)

    def ycopy(n, d, x, inward):
        there = (yy + d) % 4
        j = x * 4 + there
        return copy(
            part.at[n, j], y_recv.at[n, d - 1, x], y_ss.at[n, d, x], y_rs.at[n, d, x],
            col=xh * 4 + there,
        )

    def y_sum(n):
        for d in range(1, 4):
            for x in range(2):
                ycopy(n, d, x, True).wait_recv()

        def one(k, carry):
            at = pl.ds(pl.multiple_of(k * B, B), B)

            def total(x):
                v = part[n, x * 4 + yy, at, :].astype(F32)
                for d in range(3):
                    v = v + y_recv[n, d, x, at, :].astype(F32)
                return v

            own_sum[n, at, :] = total(xh)
            x_send[n, at, :] = total(1 - xh).astype(BF16)
            return carry

        lax.fori_loop(0, 6, one, 0)

    def xcopy(n):
        return copy(x_send.at[n], x_recv.at[n], x_ss.at[n], x_rs.at[n], col=xp)

    def samp_copy(src_of, dst_of, ss, rs, d, inward):
        there, here = (samp + d) % NS, (samp + NS - d) % NS
        return copy(src_of(there), dst_of(here if inward else samp), ss.at[d], rs.at[d], samp=there)

    def tcopy(n, d, inward):
        return samp_copy(
            lambda m: tri_send.at[m, n], lambda m: tri_recv.at[m, n], t_ss.at[n], t_rs.at[n], d, inward
        )

    lane96 = lax.broadcasted_iota(jnp.int32, (B, 128), 1)

    def triangle(n):
        xcopy(n).wait_recv()
        found = []
        for gg in range(2):
            c = []
            for q in range(3):
                at = pl.ds((gg * 3 + q) * B, B)
                c.append(own_sum[n, at, :] + x_recv[n, at, :].astype(F32))
            tail = jnp.where(
                lane96 < 32,
                pltpu.roll(c[0], 32, 1),
                jnp.where(lane96 < 64, pltpu.roll(c[1], 64, 1), pltpu.roll(c[2], 96, 1)),
            )
            found.append(c + [tail])
        for q in range(4):
            for m in range(NS):
                both = jnp.concatenate([found[0][q][m * Q : m * Q + Q], found[1][q][m * Q : m * Q + Q]], axis=0)
                tri_send[m, n, q] = both.astype(BF16)
        for d in range(1, NS):
            tcopy(n, d, False).start()

    for k in range(2 * CH + 2):
        for n in range(CH):
            t = k - 2 * n + 1
            if 1 <= t <= 4:
                for s in range(2):
                    if t > 1:
                        rcopy(n, t - 1, s, True).wait_recv()
                    rcopy(n, t, s, False).start()
                products(n, t - 1)
            elif t == 5:
                for s in range(2):
                    rcopy(n, 4, s, True).wait_recv()
                products(n, 4)
                for d in range(1, 4):
                    for x in range(2):
                        ycopy(n, d, x, False).start()
            elif t == 7:
                y_sum(n)
                xcopy(n).start()
            elif t == 8:
                triangle(n)
        if k == 0:
            for _, inc in tok_copies + cot_copies:
                inc.wait_recv()
        if k < 4:
            token_step(k)

    def kvcopy(slab, ss, rs, d, inward):
        at = slab.at[(row + NR - d) % NR if inward else row]
        return copy(at, at, ss.at[d], rs.at[d], row=(row + d) % NR)

    for d in range(1, NR):
        kvcopy(kslab, k_ss, k_rs, d, False).start()
        kvcopy(vslab, v_ss, v_rs, d, False).start()

    n = CH - 1
    for s in range(2):
        rcopy(n, 4, s, True).wait_recv()
    products(n, 4)
    for d in range(1, 4):
        for x in range(2):
            ycopy(n, d, x, False).start()
    for n in range(CH - 2, CH):
        y_sum(n)
        xcopy(n).start()
    for n in range(CH - 2, CH):
        triangle(n)

    def unpack(m):
        for n in range(CH):
            for q in range(4):
                r0 = pl.multiple_of(m * 768, 768) + (q * 4 + n) * 48
                tri_f[pl.ds(r0, 48), :] = tri_recv[m, n, q].astype(F32)

    tri_recv[samp] = tri_send[samp]
    unpack(samp)
    for d in range(1, NS):
        for n in range(CH):
            tcopy(n, d, True).wait_recv()
        unpack((samp + NS - d) % NS)

    row0 = samp * Q

    def post_step(m, carry):
        ups = []
        for e in range(4):
            i = m * 4 + e
            t = jnp.concatenate(
                [tri_f[pl.ds(i, 64, stride=48), :], tri_f[pl.ds(Q + i, 64, stride=48), :]], axis=0
            )
            center = t - jnp.mean(t, axis=0, keepdims=True)
            t = center * lax.rsqrt(jnp.mean(center * center, axis=0, keepdims=True) + 1e-05)
            proj = tn(t.astype(BF16), w_op[...])[0:B]
            at = pl.ds(pl.multiple_of((row0 + i) * B, B), B)
            gate = jax.nn.sigmoid(nn(normed[at, :], w_outgate[...]))
            ups.append((pair[at, :].astype(F32) + gate * proj).astype(BF16))
        updated = jnp.concatenate(ups, axis=0)
        trans_in = normalize(updated, ones).astype(BF16)
        total = updated.astype(F32)
        for n in range(2):
            a = nn(trans_in, w_tg[:, n * 256 : n * 256 + 256])
            u = nn(trans_in, w_tu[:, n * 256 : n * 256 + 256])
            hidden = (a * jax.nn.sigmoid(a) * u).astype(BF16)
            total = total + nn(hidden, w_td[n * 256 : n * 256 + 256, :])
        out = total.astype(BF16)
        pair_out[pl.ds(pl.multiple_of((row0 + m * 4) * B, 4 * B), 4 * B), :] = out
        bias_in = (normalize(out, ones) * lnb[...]).astype(BF16)
        for e in range(4):
            hb_send[pl.ds(m * 4 + e, 16, stride=Q), 0:B] = nt(
                wpbt[...], bias_in[e * B : e * B + B]
            ).astype(BF16).astype(F32)
        return carry

    lax.fori_loop(0, Q // 4, post_step, 0)

    def hcopy(d, inward):
        there, here = (col + d) % NC, (col + NC - d) % NC
        src = hb_send.at[pl.ds(pl.multiple_of(there * 48, 48), 48)]
        return copy(src, hb.at[here if inward else col, samp], h_ss.at[d], h_rs.at[d], col=there)

    for d in range(1, NC):
        hcopy(d, False).start()
    hb[col, samp] = hb_send[pl.ds(pl.multiple_of(col * 48, 48), 48), :]
    for d in range(1, NC):
        hcopy(d, True).wait_recv()

    def hgcopy(d, inward):
        return samp_copy(lambda _: hb.at[:, samp], lambda n: hb.at[:, n], hg_ss, hg_rs, d, inward)

    def pocopy(d, inward):
        def rows_of(n):
            return pair_out.at[pl.ds(pl.multiple_of(n * (Q * B), Q * B), Q * B)]

        return samp_copy(lambda _: rows_of(samp), rows_of, po_ss, po_rs, d, inward)

    for d in range(1, NS):
        hgcopy(d, False).start()
    for d in range(1, NS):
        pocopy(d, False).start()
    for d in range(1, NR):
        kvcopy(kslab, k_ss, k_rs, d, True).wait_recv()
        kvcopy(vslab, v_ss, v_rs, d, True).wait_recv()
    for d in range(1, NS):
        hgcopy(d, True).wait_recv()

    for b in range(NC):
        key_mask = (crop_v[0:1, b * B : b * B + B].astype(F32) - 1.0) * 10000.0
        for h in range(2):
            whole = jnp.concatenate([hb[b, n, h * Q : h * Q + Q, 0:B] for n in range(NS)], axis=0)
            bias[b, h] = whole + key_mask
            acc[b, h] = jnp.zeros((B, 128), F32)
    feature = lax.broadcasted_iota(jnp.int32, (1, B), 1)
    head_masks = [(feature < 48).astype(F32), (feature >= 48).astype(F32)]
    scale = 1.0 / math.sqrt(48)

    def att_step(s, carry):
        at = pl.ds(pl.multiple_of(s * B, B), B)
        attended = jnp.zeros((B, B), F32)
        for h in range(2):
            mask = head_masks[h].astype(BF16)
            query = q_s[at, :] * mask
            datt = datt_s[at, :] * mask
            scores = [nt(query, kslab[b, at, :]) * scale + bias[b, h] for b in range(NR)]
            top = scores[0]
            for b in range(1, NR):
                top = jnp.maximum(top, scores[b])
            top = jnp.max(top, axis=-1, keepdims=True)
            shifted = [jnp.exp(v - top) for v in scores]
            total = shifted[0]
            for b in range(1, NR):
                total = total + shifted[b]
            inv = 1.0 / jnp.sum(total, axis=-1, keepdims=True)
            probs = [v * inv for v in shifted]
            got = nn(probs[0].astype(BF16), vslab[0, at, :])
            for b in range(1, NR):
                got = got + nn(probs[b].astype(BF16), vslab[b, at, :])
            got = got * head_masks[h]
            attended = attended + got
            delta = jnp.sum(datt.astype(F32) * got, axis=-1, keepdims=True)
            for b in range(NR):
                grad = probs[b] * (nt(datt, vslab[b, at, :]) - delta)
                acc[b, h, :, 0:B] = acc[b, h, :, 0:B] + grad
        gated = (gate_s[at, :] * attended).astype(BF16)
        xd[...] = nn(gated, wo[...])
        for b in range(NC):
            pj_send[b, at, :] = xd[:, b * B : b * B + B].astype(BF16)
        return carry

    lax.fori_loop(0, 4, att_step, 0)

    def gcopy(d, inward):
        def part(n):
            return acc.at[:, :, pl.ds(pl.multiple_of(n * Q, Q), Q), :]

        return samp_copy(part, lambda n: rs_recv.at[n], g_ss, g_rs, d, inward)

    for d in range(1, NS):
        gcopy(d, False).start()
    pj_copies = [col_all(lambda n: pj_send.at[n], pj_recv, pj_ss, pj_rs, d) for d in range(1, NC)]
    for out, _ in pj_copies:
        out.start()
    for d in range(1, NS):
        gcopy(d, True).wait_recv()

    others = [(samp + d) % NS for d in range(1, NS)]

    def sum_step(b, carry):
        for h in range(2):
            total = acc[b, h, pl.ds(pl.multiple_of(samp * Q, 8), Q), :]
            for n in others:
                total = total + rs_recv[n, b, h]
            sg[b, h * Q : h * Q + Q, :] = total
        return carry

    lax.fori_loop(0, NC, sum_step, 0)

    def ccopy(d, inward):
        there, here = (col + d) % NC, (col + NC - d) % NC
        at = here if inward else col
        dst = cg.at[pl.ds(pl.multiple_of(at * 48, 48), 48)]
        return copy(sg.at[there], dst, c_ss.at[d], c_rs.at[d], col=there)

    for d in range(1, NC):
        ccopy(d, False).start()
    cg[pl.ds(pl.multiple_of(col * 48, 48), 48), :] = sg[col]
    for d in range(1, NC):
        ccopy(d, True).wait_recv()

    for i in range(Q):
        bg[samp, i] = cg[pl.ds(i, 16, stride=Q), :]

    def bcopy(d, inward):
        return samp_copy(lambda _: bg.at[samp], lambda n: bg.at[n], b_ss, b_rs, d, inward)

    for d in range(1, NS):
        bcopy(d, False).start()

    for _, inc in pj_copies:
        inc.wait_recv()
    pj_recv[col] = pj_send[col]

    def out_step(s, carry):
        at = pl.ds(pl.multiple_of(s * B, B), B)
        total = pj_recv[0, at, :].astype(F32)
        for b in range(1, NC):
            total = total + pj_recv[b, at, :].astype(F32)
        tokens_out[at, :] = (tokens[at, :].astype(F32) + total).astype(BF16)
        return carry

    lax.fori_loop(0, 4, out_step, 0)
    for d in range(1, NS):
        pocopy(d, True).wait_recv()
    for d in range(1, NS):
        bcopy(d, True).wait_recv()

    for out, _ in tok_copies + cot_copies + pj_copies:
        out.wait_send()

    for n in range(CH):
        for s in range(2):
            for t in range(1, 5):
                rcopy(n, t, s, False).wait_send()
        for d in range(1, 4):
            for x in range(2):
                ycopy(n, d, x, False).wait_send()
            tcopy(n, d, False).wait_send()
        xcopy(n).wait_send()
    for d in range(1, NR):
        kvcopy(kslab, k_ss, k_rs, d, False).wait_send()
        kvcopy(vslab, v_ss, v_rs, d, False).wait_send()
    for d in range(1, NC):
        hcopy(d, False).wait_send()
        ccopy(d, False).wait_send()
    for d in range(1, NS):
        hgcopy(d, False).wait_send()
        pocopy(d, False).wait_send()
        gcopy(d, False).wait_send()
        bcopy(d, False).wait_send()


def split(v):
    high = v.astype(BF16)
    rest = v - high.astype(F32)
    mid = rest.astype(BF16)
    return high, mid, (rest - mid.astype(F32)).astype(BF16)


def finish(pair_rows, token_rows, bg, lnb, wpbt, pair_out, tokens_out, pair_grad):
    @pl.when(pl.program_id(0) == 0)
    def _():
        tokens_out[...] = token_rows[...]

    pair_out[...] = pair_rows[...]
    ones = mean_weights()
    weights = wpbt[...].astype(F32) * lnb[...]
    weights = weights - jnp.mean(weights, axis=-1, keepdims=True)
    high, mid, low = split(weights)
    weights = jnp.concatenate([high, mid, high, mid, low, high], axis=0)
    for e in range(8):
        high, mid, low = split(bg[e])
        scaled = tn(jnp.concatenate([high, high, mid, mid, high, low], axis=0), weights)[0:B]
        center, inv = centered(pair_rows[e * B : e * B + B, :], ones)
        unit = center * inv
        pair_grad[e * B : e * B + B, :] = inv * (scaled - unit * row_means(scaled * unit, ones))


def per_device(
    pair, crop_mask, w_agate, w_aval, w_bgate, w_bval, w_outgate, w_outproj, ln_pair,
    w_trans_gate, w_trans_up, w_trans_down, ln_bias, w_pairbias, tokens, ln_token,
    w_query, w_key, w_value, w_gate, w_output, cotangent,
):
    wpbt = w_pairbias.T
    lnb = ln_bias.reshape(1, 128)
    args = (
        pair.reshape(B * B, 128), crop_mask, crop_mask.reshape(1, NC * B),
        w_agate, w_aval, w_bgate, w_bval, ln_pair.reshape(1, 128), w_outgate, w_outproj,
        w_trans_gate, w_trans_up, w_trans_down, lnb, wpbt,
        tokens.reshape(4 * B, B), cotangent.reshape(4 * B, B), ln_token.reshape(1, NC * B),
        w_query.T, w_key.T, w_value.T, w_gate.T, w_output,
    )
    vm = pltpu.VMEM
    dma = pltpu.SemaphoreType.DMA
    scratch = [
        vm((4, 128, 128), BF16),
        vm((128, 128), BF16),
        vm((B, NC * B), F32),
        vm((B, NC * B), F32),
        vm((B * B + 32, 128), BF16),
        vm((G * B, 128), F32),
        vm((G * B, 128), F32),
        vm((G, 2 * B, 128), BF16),
        vm((CH, NR, RC + 32, 128), BF16),
        vm((CH, NR, RC, 128), BF16),
        vm((CH, 3, 2, RC, 128), BF16),
        vm((CH, RC, 128), F32),
        vm((CH, RC, 128), BF16),
        vm((CH, RC, 128), BF16),
        vm((NC, 4 * B, B), BF16),
        vm((NC, 4 * B, B), BF16),
        vm((4 * B, B), BF16),
        vm((NR, 4 * B, B), BF16),
        vm((NR, 4 * B, B), BF16),
        vm((4 * B, B), F32),
        vm((4 * B, B), BF16),
        vm((NS, CH, 4, 48, 128), BF16),
        vm((NS, CH, 4, 48, 128), BF16),
        vm((64 * 48, 128), F32),
        vm((16 * Q, 128), F32),
        vm((NC, NS, 48, 128), F32),
        vm((NC, 2, B, B), F32),
        vm((NC, 2, B, 128), F32),
        vm((NC, 4 * B, B), BF16),
        vm((NC, 4 * B, B), BF16),
        vm((NS, NC, 2, Q, 128), F32),
        vm((NC, 48, 128), F32),
        vm((16 * Q, 128), F32),
    ]
    sems = [(8,)] * 4 + [(CH, 2, 4)] * 2 + [(CH, 4, 2)] * 2 + [(CH,)] * 2
    sems += [(8,)] * 4 + [(CH, 4)] * 2 + [(8,)] * 2 + [(4,)] * 4 + [(8,)] * 2 + [(4,)] * 2 + [(8,)] * 2
    sems += [(4,)] * 2
    scratch += [dma(s) for s in sems]
    spec = pl.BlockSpec(memory_space=pltpu.VMEM)
    specs = [spec] * len(args)
    specs[1] = pl.BlockSpec(memory_space=pltpu.SMEM)
    pair_rows, token_rows, bg = pl.pallas_call(
        kernel,
        out_shape=(
            jax.ShapeDtypeStruct((B * B, 128), BF16),
            jax.ShapeDtypeStruct((4 * B, B), BF16),
            jax.ShapeDtypeStruct((NS, Q, 16, 128), F32),
        ),
        in_specs=specs,
        out_specs=(spec,) * 3,
        scratch_shapes=scratch,
        compiler_params=pltpu.CompilerParams(
            collective_id=0, has_side_effects=True, vmem_limit_bytes=56 * 1024 * 1024
        ),
    )(*args)
    rows = pl.BlockSpec((8 * B, 128), lambda i: (i, 0))
    whole = pl.BlockSpec((4 * B, B), lambda i: (0, 0))
    outs = pl.pallas_call(
        finish,
        grid=(B // 8,),
        out_shape=(
            jax.ShapeDtypeStruct((B * B, 128), BF16),
            jax.ShapeDtypeStruct((4 * B, B), BF16),
            jax.ShapeDtypeStruct((B * B, 128), F32),
        ),
        in_specs=[
            rows,
            whole,
            pl.BlockSpec((8, 16, 128), lambda i: (i, 0, 0)),
            pl.BlockSpec((1, 128), lambda i: (0, 0)),
            pl.BlockSpec((16, 128), lambda i: (0, 0)),
        ],
        out_specs=(rows, whole, rows),
    )(pair_rows, token_rows, bg.reshape(B, 16, 128), lnb, wpbt)
    return (
        outs[0].reshape(B, B, 128),
        outs[1].reshape(4, B, B),
        outs[2].reshape(B, B, 128),
    )


def solution(mesh):
    placed = (
        P("row", "col", None),
        P(), P(), P(), P(), P(), P(), P(), P(), P(), P(), P(), P(), P(),
        P("samp", "row", "col"),
        P(),
        P(None, "col"),
        P(None, "col"),
        P(None, "col"),
        P(None, "col"),
        P("col", None),
        P("samp", "row", "col"),
    )
    return jax.shard_map(
        per_device,
        mesh=mesh,
        in_specs=placed,
        out_specs=(P("row", "col", None), P("samp", "row", "col"), P("row", "col", None)),
        check_vma=False,
    )
```

time: 654 us -> 236 us (0.36); the launches traced: 646 us -> 236 us
  waiting for transfers between devices: 296 us -> 0 us
  Pallas kernels: 0 us -> 233 us
  blocking collectives: 130 us -> 0 us
  matrix products: 101 us -> 0 us
  local copies, waits for them, and re-layouts: 52.7 us -> 2.53 us
  other arithmetic: 47.2 us -> 0 us
  between operations: 14.6 us -> 0.64 us
    pallas_call x0 -> x2, Pallas kernels: none -> 233 us  [the longest x1 202 us: per_device(): pl.pallas_call(kernel, out_shape=(jax.ShapeDtypeStruct((B * B, 128), BF16...]
    unnamed x7 -> x0, waiting for transfers between devices: 167 us -> none
    all_gather x4 -> x0, blocking collectives: 110 us -> none  [the longest x1 33.4 us: per_device(): lax.all_gather(tokens, 'col', axis=2, tiled=True)]
    dot_general x33 -> x0, matrix products: 97.1 us -> none  [the longest x8 23.2 us: pair_transition(): jnp.dot(hidden, w_trans_down, preferred_element_type=jnp.float32)]
    all_gather x2 -> x0, waiting for transfers between devices: 70.1 us -> none  [the longest x1 70.1 us: per_device(): lax.all_gather(right, 'row', axis=0, tiled=True)]
    psum x1 -> x0, waiting for transfers between devices: 59.7 us -> none  [per_device(): summed_grad = lax.psum(local_grad, 'samp')]
    reduce_sum x24 -> x0, other arithmetic: 36.8 us -> none  [the longest x11 15.9 us: normalize(): jnp.mean(center * center, axis=-1, keepdims=True) + 1e-05]
    unnamed x72 -> x0, local copies, waits for them, and re-layouts: 35.8 us -> none
  transfers between devices with their start and end apart: 6 -> 0, of which waited for: 4 -> 0; matrix products, arithmetic and copies ran while one was open for 8% -> 0% of each run, Pallas kernels for 0% -> 0%
where the time goes in v1:
time: 236 us
  Pallas kernels  233 us (99%)
  local copies, waits for them, and re-layouts  2.53 us (1%)
    pallas_call x1, Pallas kernels, per_device(): pl.pallas_call(kernel, out_shape=(jax.ShapeDtypeStruct((B * B, 128), BF16...  202 us
    pallas_call x1, Pallas kernels, per_device(): pl.pallas_call(finish, grid=(B // 8,), out_shape=(jax.ShapeDtypeStruct((B...  30.8 us

profile of v1, /device:TPU:1, one launch (start us, length us, event | category | flops | bytes accessed | tf_op | source)
XLA Modules:
  0.0 236.1 jit_solution(17662020125484213137)
XLA Ops:
  0.6 1.3 reshape.45.lnt
  1.9 1.3 reshape.40.crop_v
  3.2 202.1 %shard_map.229 = (bf16[9216,128]{1,0:T(8,128)(2,1)}, bf16[384,96]{1,0:T(8,128)(2,1)}, f32[4,24,16,128]{3,2,1,0:T(8,128)}) custom-call(bf16[9216,128]{1,0:T(8,128)(2,1)} %bitcast.14, s32[768]{0:T(1024)} %crop_s.1, s32[1,768]{1,0:T(1,128)} %reshape.40.crop_v, bf16[128,128]{1,0:T(8,128)(2,1)} %w_ag.1, bf16[128,128]{1,0:T(8,128)(2,1)} %w_av.1, ...), custom_call_target="tpu_custom_call" | custom-call | tf_op jit(solution)/shard_map/pallas_call | solution.py:625
  205.3 30.8 %shard_map.230 = (bf16[9216,128]{1,0:T(8,128)(2,1)}, bf16[384,96]{1,0:T(8,128)(2,1)}, f32[9216,128]{1,0:T(8,128)}) custom-call(bf16[9216,128]{1,0:T(8,128)(2,1)} %get-tuple-element.9.pair_rows, bf16[384,96]{1,0:T(8,128)(2,1)} %get-tuple-element.10.token_rows, f32[96,16,128]{2,1,0:T(8,128)} %bitcast.15, f32[1,128]{1,0:T(1,128)} %bitcast.25, ...), custom_call_target="tpu_custom_call" | custom-call | tf_op jit(solution)/shard_map/pallas_call | solution.py:641

commit v2 on v1

v2 whole, which is shorter than its diff:
```python
import math

import jax
import jax.numpy as jnp
from jax import lax
from jax.experimental import pallas as pl
from jax.experimental.pallas import tpu as pltpu
from jax.sharding import PartitionSpec as P

F32 = jnp.float32
BF16 = jnp.bfloat16
MESH = pl.DeviceIdType.MESH
NR = 8
NC = 8
NS = 4
B = 96
Q = 24
G = 24
CH = 8
RC = 3 * B


def nt(a, b):
    return lax.dot_general(a, b, (((1,), (1,)), ((), ())), preferred_element_type=F32)


def nn(a, b):
    return lax.dot_general(a, b, (((1,), (0,)), ((), ())), preferred_element_type=F32)


def tn(a, b):
    return lax.dot_general(a, b, (((0,), (0,)), ((), ())), preferred_element_type=F32)


def row_means(values, ones):
    high = values.astype(BF16)
    low = (values - high.astype(F32)).astype(BF16)
    return nn(jnp.concatenate([high, low], axis=1), ones)


def centered(values, ones):
    center = values.astype(F32) - nn(values, ones[0:128])
    return center, lax.rsqrt(row_means(center * center, ones) + 1e-05)


def normalize(values, ones):
    center, inv = centered(values, ones)
    return center * inv


def mean_weights():
    return jnp.full((256, 128), 1.0 / 128.0, BF16)


def kernel(
    pair, crop_s, crop_v, w_ag, w_av, w_bg, w_bv, lnp, w_outgate, w_outproj, w_tg, w_tu, w_td,
    lnb, wpbt, tokens, cot, lnt, wq, wk, wv, wg, wo,
    pair_out, tokens_out, bg,
    wt, w_op, xd, cd,
    normed, lf, rf, lm, rslab, part, z_recv, y_recv, own_sum, x_send, x_recv, slab, q_s, kslab,
    vslab, gate_s, datt_s, tri_send, tri_recv, tri_f, hb_f, hb_send, hb, bias, acc, g_send, g_recv,
    pj_send, py_recv, px_own, px_send, px_recv, sg, cg, cg_f,
    slab_ss, slab_rs, ring_ss, ring_rs, z_ss, z_rs, y_ss, y_rs, x_ss, x_rs,
    k_ss, k_rs, v_ss, v_rs, t_ss, t_rs, h_ss, h_rs, hg_ss, hg_rs, po_ss, po_rs, pr_ss, pr_rs,
    py_ss, py_rs, px_ss, px_rs, g_ss, g_rs, c_ss, c_rs, b_ss, b_rs,
):
    row = lax.axis_index("row")
    col = lax.axis_index("col")
    samp = lax.axis_index("samp")
    xh = col // 4
    yy = col % 4
    xp = (1 - xh) * 4 + yy
    ones = mean_weights()
    right = (row + 1) % NR
    left = (row + NR - 1) % NR

    def copy(src, dst, ss, rs, **where):
        return pltpu.make_async_remote_copy(
            src_ref=src, dst_ref=dst, send_sem=ss, recv_sem=rs, device_id=where, device_id_type=MESH
        )

    barrier = pltpu.get_barrier_semaphore()
    for d in range(1, NC):
        pl.semaphore_signal(barrier, inc=1, device_id={"col": (col + d) % NC}, device_id_type=MESH)
    for d in range(1, NR):
        pl.semaphore_signal(barrier, inc=1, device_id={"row": (row + d) % NR}, device_id_type=MESH)
    for d in range(1, NS):
        pl.semaphore_signal(
            barrier, inc=1, device_id={"samp": (samp + d) % NS}, device_id_type=MESH
        )

    pl.semaphore_wait(barrier, NC + NR + NS - 3)

    def around(d):
        return (yy + d) % 4

    def slab_copy(block, k, there):
        at = slab.at[block]
        return copy(at, at, slab_ss.at[k], slab_rs.at[k], col=there)

    slab_own = [slab_copy(col, d, xh * 4 + around(d)) for d in range(1, 4)]
    slab_own_in = [slab_copy(xh * 4 + around(4 - d), d, xh * 4 + around(d)) for d in range(1, 4)]
    slab_x = slab_copy(col, 0, xp)
    slab_x_in = slab_copy(xp, 0, xp)
    slab_on = [slab_copy(xp, 3 + d, xh * 4 + around(d)) for d in range(1, 4)]
    slab_on_in = [
        slab_copy((1 - xh) * 4 + around(4 - d), 3 + d, xh * 4 + around(d)) for d in range(1, 4)
    ]
    slab[col, 0] = tokens[...]
    slab[col, 1] = cot[...]
    for c in [slab_x] + slab_own:
        c.start()

    for n, w in enumerate((w_ag, w_av, w_bg, w_bv)):
        wt[n] = w[...].astype(F32).T.astype(BF16)
    wp = jnp.concatenate([wt[n, pl.ds(pl.multiple_of(samp * 32, 32), 32), :] for n in range(4)], axis=0)
    tri_f[0:128, :] = w_outproj[...].astype(F32)
    w_op[...] = jnp.concatenate(
        [tri_f[pl.ds(0, 64, stride=2), :], tri_f[pl.ds(1, 64, stride=2), :]], axis=0
    ).astype(BF16)
    keep_cols = jnp.zeros((1, B), F32)
    for b in range(NC):
        here = crop_v[0:1, b * B : b * B + B].astype(F32)
        keep_cols = jnp.where(col == b, here, keep_cols)
    keep_cols = jnp.concatenate([keep_cols, jnp.zeros((1, 32), F32)], axis=1)

    def norm_step(m, carry):
        for e in range(4):
            at = pl.ds(pl.multiple_of(m * 1536 + e * 384, 384), 384)
            normed[at, :] = (normalize(pair[at, :], ones) * lnp[...]).astype(BF16)
        return carry

    lax.fori_loop(0, 6, norm_step, 0)
    slab_x_in.wait_recv()
    for c in slab_on:
        c.start()
    normed[B * B : B * B + 32, :] = jnp.zeros((32, 128), BF16)
    lane = lax.broadcasted_iota(jnp.int32, (8, 128), 1)
    wide = lane < B

    def edges(weights, dest):
        def step(m, carry):
            for e in range(8):
                i = m * 8 + e
                rows = normed[pl.ds(pl.multiple_of(i * B, 32), 128), :]
                o = nt(weights, rows)
                kept = keep_cols * crop_s[row * B + i].astype(F32)
                edge = jax.nn.sigmoid(o[0:32]) * o[32:64] * kept
                tail = edge[24:32]
                for q in range(3):
                    packed = jnp.where(
                        wide, edge[8 * q : 8 * q + 8], pltpu.roll(tail, 96 - 32 * q, 1)
                    )
                    dest[pl.ds(i + 8 * B * q, 8, stride=B), :] = packed
            return carry

        lax.fori_loop(0, B // 8, step, 0)

    edges(wp[64:128], rf)
    own = lax.broadcasted_iota(jnp.int32, (B, 128), 1) < B
    carriers = [(n, k, pl.ds((k * 8 + n) * B, B)) for n in range(CH) for k in range(3)]
    for n, k, at in carriers:
        rslab[n, row, k * B : k * B + B, :] = rf[at, :].astype(BF16)
    for n in range(CH):
        rslab[n, :, RC : RC + 32, :] = jnp.zeros((NR, 32, 128), BF16)

    ring = (right, left)
    step_of = (-1, 1)

    def rcopy(n, t, s, inward):
        back = t if inward else t - 1
        block = (row + NR + step_of[s] * back) % NR
        rows = pl.ds(0, RC) if t < 4 else pl.ds(s * (RC // 2), RC // 2)
        at = rslab.at[n, block, rows]
        return copy(at, at, ring_ss.at[n, s, t - 1], ring_rs.at[n, s, t - 1], row=ring[s])

    for n in range(3):
        for s in range(2):
            rcopy(n, 1, s, False).start()
    edges(wp[0:64], lf)
    for n, k, at in carriers:
        edge = lf[at, :]
        lm[3 * n + k, 0:B, :] = jnp.where(own, edge, 0.0).astype(BF16)
        lm[3 * n + k, B : 2 * B, :] = jnp.where(own, 0.0, edge).astype(BF16)

    def token_step(pair_of):
        at = pl.ds(pair_of * 2 * B, 2 * B)
        x = [slab[b, 0, at, :].astype(F32) for b in range(NC)]
        total = x[0]
        for b in range(1, NC):
            total = total + x[b]
        mean = jnp.sum(total, axis=-1, keepdims=True) * (1.0 / (NC * B))
        x = [v - mean for v in x]
        total = x[0] * x[0]
        for b in range(1, NC):
            total = total + x[b] * x[b]
        inv = lax.rsqrt(jnp.sum(total, axis=-1, keepdims=True) * (1.0 / (NC * B)) + 1e-05)
        for b in range(NC):
            xd[:, b * B : b * B + B] = x[b] * inv
            cd[:, b * B : b * B + B] = slab[b, 1, at, :].astype(F32)
        normal = (xd[...] * lnt[...]).astype(BF16)
        q_s[at, :] = nt(normal, wq[...]).astype(BF16)
        tokens_at = pl.ds(pl.multiple_of(row * B, B), B)
        for w, dest in ((wk, kslab), (wv, vslab)):
            out = nt(normal, w[...]).astype(BF16)
            for e in range(2):
                dest[pair_of * 2 + e, tokens_at, :] = out[e * B : e * B + B]
        gate = jax.nn.sigmoid(nt(normal, wg[...]))
        gate_s[at, :] = gate
        d = nt(cd[...].astype(BF16), wo[...])
        datt_s[at, :] = (d * gate).astype(BF16)

    def product(n, j):
        tops, tail = [], None
        for q in range(3):
            o = nt(lm[3 * n + q], rslab[n, j, q * B : q * B + 128, :])
            tops.append(o[0:B])
            tail = o[B : 2 * B] if tail is None else tail + o[B : 2 * B]
        for q in range(3):
            packed = jnp.where(own, tops[q], pltpu.roll(tail, 96 - 32 * q, 1))
            part[n, j, q * B : q * B + B, :] = packed.astype(BF16)

    def products(n, back):
        if back in (0, 4):
            product(n, (row + back) % NR)
        else:

            def one(d, carry):
                product(n, (row + NR + (2 * d - 1) * back) % NR)
                return carry

            lax.fori_loop(0, 2, one, 0)

    sides = (xh * 4 + (yy + 1) % 4, xh * 4 + (yy + 3) % 4)

    def zcopy(n, s, x):
        src = part.at[n, x * 4 + (yy + 2) % 4, pl.ds(s * (RC // 2), RC // 2)]
        return copy(src, z_recv.at[n, s, x], z_ss.at[n, s, x], z_rs.at[n, s, x], col=sides[s])

    def ycopy(n, s, x):
        src = part.at[n, x * 4 + (yy + 1 + 2 * s) % 4]
        return copy(src, y_recv.at[n, s, x], y_ss.at[n, s, x], y_rs.at[n, s, x], col=sides[s])

    each = [(s, x) for s in range(2) for x in range(2)]

    def z_start(n):
        for s, x in each:
            zcopy(n, s, x).start()

    def y_start(n):
        for s, x in each:
            zcopy(n, s, x).wait_recv()
            j = x * 4 + (yy + 1 + 2 * s) % 4
            at = pl.ds(s * (RC // 2), RC // 2)
            more = z_recv[n, s, x].astype(F32)
            part[n, j, at, :] = (part[n, j, at, :].astype(F32) + more).astype(BF16)
            ycopy(n, s, x).start()

    def y_sum(n):
        for s, x in each:
            ycopy(n, s, x).wait_recv()

        def one(k, carry):
            at = pl.ds(pl.multiple_of(k * B, B), B)

            def total(x):
                v = part[n, x * 4 + yy, at, :].astype(F32)
                for s in range(2):
                    v = v + y_recv[n, s, x, at, :].astype(F32)
                return v

            own_sum[n, at, :] = total(xh)
            x_send[n, at, :] = total(1 - xh).astype(BF16)
            return carry

        lax.fori_loop(0, 3, one, 0)
        xcopy(n).start()

    def xcopy(n):
        return copy(x_send.at[n], x_recv.at[n], x_ss.at[n], x_rs.at[n], col=xp)

    def samp_copy(src_of, dst_of, ss, rs, d, inward):
        there, here = (samp + d) % NS, (samp + NS - d) % NS
        return copy(src_of(there), dst_of(here if inward else samp), ss.at[d], rs.at[d], samp=there)

    def tcopy(n, d, inward):
        return samp_copy(
            lambda m: tri_send.at[m, n], lambda m: tri_recv.at[m, n], t_ss.at[n], t_rs.at[n], d, inward
        )

    lane96 = lax.broadcasted_iota(jnp.int32, (B, 128), 1)

    def triangle(n):
        xcopy(n).wait_recv()
        c = []
        for q in range(3):
            at = pl.ds(q * B, B)
            c.append(own_sum[n, at, :] + x_recv[n, at, :].astype(F32))
        tail = jnp.where(
            lane96 < 32,
            pltpu.roll(c[0], 32, 1),
            jnp.where(lane96 < 64, pltpu.roll(c[1], 64, 1), pltpu.roll(c[2], 96, 1)),
        )
        c.append(tail)
        for h in range(2):
            for m in range(NS):
                both = [v[m * Q : m * Q + Q] for v in c[2 * h : 2 * h + 2]]
                tri_send[m, n, h] = jnp.concatenate(both, axis=0).astype(BF16)
        for d in range(1, NS):
            tcopy(n, d, False).start()

    def kvcopy(slab, ss, rs, d, inward):
        block = (row + NR - d) % NR if inward else row
        at = slab.at[:, pl.ds(pl.multiple_of(block * B, B), B), :]
        return copy(at, at, ss.at[d], rs.at[d], row=(row + d) % NR)

    for k in range(CH + 7):
        active = [(n, k - n + 1) for n in range(CH)]
        for n, t in active:
            if 1 <= t <= 5:
                for s in range(2):
                    if t > 1:
                        rcopy(n, t - 1, s, True).wait_recv()
                    if t < 5 and not (t == 1 and n < 3):
                        rcopy(n, t, s, False).start()
        if k == CH + 2:
            for d in range(1, NR):
                kvcopy(kslab, k_ss, k_rs, d, False).start()
                kvcopy(vslab, v_ss, v_rs, d, False).start()
        for n, t in active:
            if t == 5:
                products(n, 4)
                z_start(n)
            elif t == 6:
                y_start(n)
            elif t == 7:
                y_sum(n)
            elif t == 8:
                triangle(n)
        for n, t in active:
            if 1 <= t <= 4:
                products(n, t - 1)
        if k == 1:
            for c in slab_own_in + slab_on_in:
                c.wait_recv()
        if k in (1, 3):
            token_step(k // 2)

    def unpack(m):
        for n in range(CH):
            for h in range(2):
                both = tri_recv[m, n, h].astype(F32)
                for e in range(2):
                    c = (2 * h + e) * 8 + n
                    r0 = pl.multiple_of(m * 768, 768) + c // 2 * 48 + c % 2 * Q
                    tri_f[pl.ds(r0, Q), :] = both[e * Q : e * Q + Q]

    tri_recv[samp] = tri_send[samp]
    unpack(samp)
    for d in range(1, NS):
        for n in range(CH):
            tcopy(n, d, True).wait_recv()
        unpack((samp + NS - d) % NS)

    row0 = samp * Q
    sib, oth = samp + 1 - 2 * (samp % 2), (samp + 2) % NS
    diag = (sib + 2) % NS

    def part_of(n, m):
        return pair_out.at[pl.ds(pl.multiple_of((n * Q + m * 4) * B, 4 * B), 4 * B)]

    def pocopy(k, m, inward):
        there = (sib, oth)[k]
        at = part_of(there if inward else samp, m)
        return copy(at, at, po_ss.at[k, m], po_rs.at[k, m], samp=there)

    def prcopy(inward):
        n = diag if inward else oth
        at = pair_out.at[pl.ds(pl.multiple_of(n * (Q * B), Q * B), Q * B)]
        return copy(at, at, pr_ss, pr_rs, samp=sib)


    def post_step(m, carry):
        cols = []
        for e in range(4):
            i = m * 4 + e
            cols.append(
                jnp.concatenate(
                    [tri_f[pl.ds(i, 64, stride=48), :], tri_f[pl.ds(Q + i, 64, stride=48), :]], axis=0
                )
            )
        t = jnp.concatenate(cols, axis=1)
        center = t - jnp.mean(t, axis=0, keepdims=True)
        t = center * lax.rsqrt(jnp.mean(center * center, axis=0, keepdims=True) + 1e-05)
        proj = tn(t.astype(BF16), w_op[...])
        proj = jnp.concatenate([proj[e * 128 : e * 128 + B] for e in range(4)], axis=0)
        at = pl.ds(pl.multiple_of((row0 + m * 4) * B, 4 * B), 4 * B)
        gate = jax.nn.sigmoid(nn(normed[at, :], w_outgate[...]))
        updated = (pair[at, :].astype(F32) + gate * proj).astype(BF16)
        trans_in = normalize(updated, ones).astype(BF16)
        total = updated.astype(F32)
        for n in range(2):
            a = nn(trans_in, w_tg[:, n * 256 : n * 256 + 256])
            u = nn(trans_in, w_tu[:, n * 256 : n * 256 + 256])
            hidden = (a * jax.nn.sigmoid(a) * u).astype(BF16)
            total = total + nn(hidden, w_td[n * 256 : n * 256 + 256, :])
        out = total.astype(BF16)
        pair_out[at, :] = out
        for k in range(2):
            pocopy(k, m, False).start()
        bias_in = (normalize(out, ones) * lnb[...]).astype(BF16)
        o = nt(wpbt[...], bias_in)
        for e in range(4):
            hb_f[pl.ds(m * 4 + e, 16, stride=Q), 0:B] = o[:, e * B : e * B + B]
        return carry

    lax.fori_loop(0, Q // 4, post_step, 0)

    for c in range(NC):
        hb_send[c] = hb_f[c * 48 : c * 48 + 48, :].astype(BF16)

    def hcopy(d, inward):
        there, here = (col + d) % NC, (col + NC - d) % NC
        dst = hb.at[here if inward else col, samp]
        return copy(hb_send.at[there], dst, h_ss.at[d], h_rs.at[d], col=there)

    for d in range(1, NC):
        hcopy(d, False).start()
    hb[col, samp] = hb_send[col]
    for d in range(1, NC):
        hcopy(d, True).wait_recv()

    def hgcopy(d, inward):
        return samp_copy(lambda _: hb.at[:, samp], lambda n: hb.at[:, n], hg_ss, hg_rs, d, inward)

    for d in range(1, NS):
        hgcopy(d, False).start()
    for d in range(1, NR):
        kvcopy(kslab, k_ss, k_rs, d, True).wait_recv()
        kvcopy(vslab, v_ss, v_rs, d, True).wait_recv()
    for d in range(1, NS):
        hgcopy(d, True).wait_recv()

    for b in range(NC):
        key_mask = (crop_v[0:1, b * B : b * B + B].astype(F32) - 1.0) * 10000.0
        quarters = [hb[b, n].astype(F32) for n in range(NS)]
        for h in range(2):
            whole = jnp.concatenate([v[h * Q : h * Q + Q, 0:B] for v in quarters], axis=0)
            bias[h * B : h * B + B, b * B : b * B + B] = whole + key_mask
    acc[...] = jnp.zeros((2 * B, NC * B), F32)
    feature = lax.broadcasted_iota(jnp.int32, (1, B), 1)
    head_masks = [(feature < 48).astype(F32), (feature >= 48).astype(F32)]
    scale = 1.0 / math.sqrt(48)

    def att_step(s, carry):
        at = pl.ds(pl.multiple_of(s * B, B), B)
        query, datt = q_s[at, :], datt_s[at, :]
        query = jnp.concatenate([query * m.astype(BF16) for m in head_masks], axis=0)
        datt = jnp.concatenate([datt * m.astype(BF16) for m in head_masks], axis=0)
        scores = nt(query, kslab[s]) * scale + bias[...]
        shifted = jnp.exp(scores - jnp.max(scores, axis=-1, keepdims=True))
        probs = shifted * (1.0 / jnp.sum(shifted, axis=-1, keepdims=True))
        got = nn(probs.astype(BF16), vslab[s])
        delta = jnp.sum(datt.astype(F32) * got, axis=-1, keepdims=True)
        acc[...] = acc[...] + probs * (nt(datt, vslab[s]) - delta)
        attended = got[0:B] * head_masks[0] + got[B : 2 * B] * head_masks[1]
        gated = (gate_s[at, :] * attended).astype(BF16)
        xd[0:B, :] = nn(gated, wo[...])
        for b in range(NC):
            pj_send[b, at, :] = xd[0:B, b * B : b * B + B].astype(BF16)
        return carry

    lax.fori_loop(0, 4, att_step, 0)
    for m in range(6):
        pocopy(1, m, True).wait_recv()
    prcopy(False).start()

    for b in range(NC):
        heads = [acc[h * B : h * B + B, b * B : b * B + B] for h in range(2)]
        for n in range(NS):
            both = jnp.concatenate([v[n * Q : n * Q + Q] for v in heads], axis=0)
            g_send[n, b, :, 0:B] = both.astype(BF16)

    def gcopy(d, inward):
        return samp_copy(lambda n: g_send.at[n], lambda n: g_recv.at[n], g_ss, g_rs, d, inward)

    for d in range(1, NS):
        gcopy(d, False).start()

    def pycopy(d, x):
        src = pj_send.at[x * 4 + around(d)]
        return copy(src, py_recv.at[d - 1, x], py_ss.at[d, x], py_rs.at[d, x], col=xh * 4 + around(d))

    pys = [(d, x) for d in range(1, 4) for x in range(2)]
    for d, x in pys:
        pycopy(d, x).start()
    g_recv[samp] = g_send[samp]
    for d in range(1, NS):
        gcopy(d, True).wait_recv()

    def sum_step(b, carry):
        total = g_recv[0, b].astype(F32)
        for n in range(1, NS):
            total = total + g_recv[n, b].astype(F32)
        sg[b] = total.astype(BF16)
        return carry

    lax.fori_loop(0, NC, sum_step, 0)

    def ccopy(d, inward):
        there, here = (col + d) % NC, (col + NC - d) % NC
        return copy(sg.at[there], cg.at[here if inward else col], c_ss.at[d], c_rs.at[d], col=there)

    for d in range(1, NC):
        ccopy(d, False).start()
    cg[col] = sg[col]

    for d, x in pys:
        pycopy(d, x).wait_recv()

    def py_step(s, carry):
        at = pl.ds(pl.multiple_of(s * B, B), B)

        def total(x):
            v = pj_send[x * 4 + yy, at, :].astype(F32)
            for d in range(3):
                v = v + py_recv[d, x, at, :].astype(F32)
            return v

        px_own[at, :] = total(xh) + tokens[at, :].astype(F32)
        px_send[at, :] = total(1 - xh).astype(BF16)
        return carry

    lax.fori_loop(0, 4, py_step, 0)
    px = copy(px_send, px_recv, px_ss, px_rs, col=xp)
    px.start()
    for d in range(1, NC):
        ccopy(d, True).wait_recv()
    for c in range(NC):
        cg_f[c * 48 : c * 48 + 48, :] = cg[c].astype(F32)
    for i in range(Q):
        bg[samp, i] = cg_f[pl.ds(i, 16, stride=Q), :].astype(BF16)

    def bcopy(d, inward):
        return samp_copy(lambda _: bg.at[samp], lambda n: bg.at[n], b_ss, b_rs, d, inward)

    for d in range(1, NS):
        bcopy(d, False).start()
    px.wait_recv()
    tokens_out[...] = (px_own[...] + px_recv[...].astype(F32)).astype(BF16)
    for m in range(6):
        pocopy(0, m, True).wait_recv()
    prcopy(True).wait_recv()
    for d in range(1, NS):
        bcopy(d, True).wait_recv()

    for c in [slab_x, px, prcopy(False)] + slab_own + slab_on:
        c.wait_send()
    for d, x in pys:
        pycopy(d, x).wait_send()
    for m in range(6):
        for k in range(2):
            pocopy(k, m, False).wait_send()

    for n in range(CH):
        for s in range(2):
            for t in range(1, 5):
                rcopy(n, t, s, False).wait_send()
        for s, x in each:
            zcopy(n, s, x).wait_send()
            ycopy(n, s, x).wait_send()
        for d in range(1, NS):
            tcopy(n, d, False).wait_send()
        xcopy(n).wait_send()
    for d in range(1, NR):
        kvcopy(kslab, k_ss, k_rs, d, False).wait_send()
        kvcopy(vslab, v_ss, v_rs, d, False).wait_send()
    for d in range(1, NC):
        hcopy(d, False).wait_send()
        ccopy(d, False).wait_send()
    for d in range(1, NS):
        hgcopy(d, False).wait_send()
        gcopy(d, False).wait_send()
        bcopy(d, False).wait_send()


def split(v):
    high = v.astype(BF16)
    rest = v - high.astype(F32)
    mid = rest.astype(BF16)
    return high, mid, (rest - mid.astype(F32)).astype(BF16)


def finish(pair_rows, token_rows, bg, lnb, wpbt, pair_out, tokens_out, pair_grad):
    @pl.when(pl.program_id(0) == 0)
    def _():
        tokens_out[...] = token_rows[...]

    pair_out[...] = pair_rows[...]
    ones = mean_weights()
    weights = wpbt[...].astype(F32) * lnb[...]
    weights = weights - jnp.mean(weights, axis=-1, keepdims=True)
    weights = jnp.concatenate(split(weights), axis=0)
    for e in range(2):
        at = slice(e * 4 * B, e * 4 * B + 4 * B)
        grads = jnp.concatenate([bg[e * 4 + i] for i in range(4)], axis=1)
        scaled = tn(jnp.concatenate([grads, grads, grads], axis=0), weights)
        scaled = jnp.concatenate([scaled[i * 128 : i * 128 + B] for i in range(4)], axis=0)
        center, inv = centered(pair_rows[at, :], ones)
        unit = center * inv
        pair_grad[at, :] = inv * (scaled - unit * row_means(scaled * unit, ones))


def per_device(
    pair, crop_mask, w_agate, w_aval, w_bgate, w_bval, w_outgate, w_outproj, ln_pair,
    w_trans_gate, w_trans_up, w_trans_down, ln_bias, w_pairbias, tokens, ln_token,
    w_query, w_key, w_value, w_gate, w_output, cotangent,
):
    wpbt = w_pairbias.T
    lnb = ln_bias.reshape(1, 128)
    args = (
        pair.reshape(B * B, 128), crop_mask, crop_mask.reshape(1, NC * B),
        w_agate, w_aval, w_bgate, w_bval, ln_pair.reshape(1, 128), w_outgate, w_outproj,
        w_trans_gate, w_trans_up, w_trans_down, lnb, wpbt,
        tokens.reshape(4 * B, B), cotangent.reshape(4 * B, B), ln_token.reshape(1, NC * B),
        w_query.T, w_key.T, w_value.T, w_gate.T, w_output,
    )
    vm = pltpu.VMEM
    dma = pltpu.SemaphoreType.DMA
    scratch = [
        vm((4, 128, 128), BF16),
        vm((128, 128), BF16),
        vm((2 * B, NC * B), F32),
        vm((2 * B, NC * B), F32),
        vm((B * B + 32, 128), BF16),
        vm((G * B, 128), F32),
        vm((G * B, 128), F32),
        vm((G, 2 * B, 128), BF16),
        vm((CH, NR, RC + 32, 128), BF16),
        vm((CH, NR, RC, 128), BF16),
        vm((CH, 2, 2, RC // 2, 128), BF16),
        vm((CH, 2, 2, RC, 128), BF16),
        vm((CH, RC, 128), F32),
        vm((CH, RC, 128), BF16),
        vm((CH, RC, 128), BF16),
        vm((NC, 2, 4 * B, B), BF16),
        vm((4 * B, B), BF16),
        vm((4, NR * B, B), BF16),
        vm((4, NR * B, B), BF16),
        vm((4 * B, B), F32),
        vm((4 * B, B), BF16),
        vm((NS, CH, 2, 48, 128), BF16),
        vm((NS, CH, 2, 48, 128), BF16),
        vm((64 * 48, 128), F32),
        vm((16 * Q, 128), F32),
        vm((NC, 48, 128), BF16),
        vm((NC, NS, 48, 128), BF16),
        vm((2 * B, NC * B), F32),
        vm((2 * B, NC * B), F32),
        vm((NS, NC, 48, 128), BF16),
        vm((NS, NC, 48, 128), BF16),
        vm((NC, 4 * B, B), BF16),
        vm((3, 2, 4 * B, B), BF16),
        vm((4 * B, B), F32),
        vm((4 * B, B), BF16),
        vm((4 * B, B), BF16),
        vm((NC, 48, 128), BF16),
        vm((NC, 48, 128), BF16),
        vm((16 * Q, 128), F32),
    ]
    sems = [(7,)] * 2 + [(CH, 2, 4)] * 2 + [(CH, 2, 2)] * 4 + [(CH,)] * 2
    sems += [(8,)] * 4 + [(CH, 4)] * 2 + [(8,)] * 2 + [(4,)] * 2 + [(2, 6)] * 2 + [None] * 2
    sems += [(4, 2)] * 2 + [None] * 2 + [(4,)] * 2 + [(8,)] * 2 + [(4,)] * 2
    scratch += [dma if s is None else dma(s) for s in sems]
    spec = pl.BlockSpec(memory_space=pltpu.VMEM)
    specs = [spec] * len(args)
    specs[1] = pl.BlockSpec(memory_space=pltpu.SMEM)
    pair_rows, token_rows, bg = pl.pallas_call(
        kernel,
        out_shape=(
            jax.ShapeDtypeStruct((B * B, 128), BF16),
            jax.ShapeDtypeStruct((4 * B, B), BF16),
            jax.ShapeDtypeStruct((NS, Q, 16, 128), BF16),
        ),
        in_specs=specs,
        out_specs=(spec,) * 3,
        scratch_shapes=scratch,
        compiler_params=pltpu.CompilerParams(
            collective_id=0, has_side_effects=True, vmem_limit_bytes=56 * 1024 * 1024
        ),
    )(*args)
    rows = pl.BlockSpec((8 * B, 128), lambda i: (i, 0))
    whole = pl.BlockSpec((4 * B, B), lambda i: (0, 0))
    outs = pl.pallas_call(
        finish,
        grid=(B // 8,),
        out_shape=(
            jax.ShapeDtypeStruct((B * B, 128), BF16),
            jax.ShapeDtypeStruct((4 * B, B), BF16),
            jax.ShapeDtypeStruct((B * B, 128), F32),
        ),
        in_specs=[
            rows,
            whole,
            pl.BlockSpec((8, 16, 128), lambda i: (i, 0, 0)),
            pl.BlockSpec((1, 128), lambda i: (0, 0)),
            pl.BlockSpec((16, 128), lambda i: (0, 0)),
        ],
        out_specs=(rows, whole, rows),
    )(pair_rows, token_rows, bg.reshape(B, 16, 128), lnb, wpbt)
    return (
        outs[0].reshape(B, B, 128),
        outs[1].reshape(4, B, B),
        outs[2].reshape(B, B, 128),
    )


def solution(mesh):
    placed = (
        P("row", "col", None),
        P(), P(), P(), P(), P(), P(), P(), P(), P(), P(), P(), P(), P(),
        P("samp", "row", "col"),
        P(),
        P(None, "col"),
        P(None, "col"),
        P(None, "col"),
        P(None, "col"),
        P("col", None),
        P("samp", "row", "col"),
    )
    return jax.shard_map(
        per_device,
        mesh=mesh,
        in_specs=placed,
        out_specs=(P("row", "col", None), P("samp", "row", "col"), P("row", "col", None)),
        check_vma=False,
    )
```

time: 236 us -> 182 us (0.77)
  Pallas kernels: 233 us -> 179 us
    pallas_call x1, Pallas kernels: 202 us -> 165 us  [per_device(): pl.pallas_call(kernel, out_shape=(jax.ShapeDtypeStruct((B * B, 128), BF16...]
    pallas_call x1, Pallas kernels: 30.8 us -> 13.4 us  [per_device(): pl.pallas_call(finish, grid=(B // 8,), out_shape=(jax.ShapeDtypeStruct((B...]
where the time goes in v2:
time: 182 us
  Pallas kernels  179 us (98%)
  local copies, waits for them, and re-layouts  2.53 us (1%)
    pallas_call x1, Pallas kernels, per_device(): pl.pallas_call(kernel, out_shape=(jax.ShapeDtypeStruct((B * B, 128), BF16...  165 us
    pallas_call x1, Pallas kernels, per_device(): pl.pallas_call(finish, grid=(B // 8,), out_shape=(jax.ShapeDtypeStruct((B...  13.4 us

profile of v2, /device:TPU:1, one launch (start us, length us, event | category | flops | bytes accessed | tf_op | source)
XLA Modules:
  0.0 181.8 jit_solution(5690992964940588736)
XLA Ops:
  0.6 1.3 reshape.45.lnt
  1.9 1.3 reshape.40.crop_v
  3.2 165.2 %shard_map.229 = (bf16[9216,128]{1,0:T(8,128)(2,1)}, bf16[384,96]{1,0:T(8,128)(2,1)}, bf16[4,24,16,128]{3,2,1,0:T(8,128)(2,1)}) custom-call(bf16[9216,128]{1,0:T(8,128)(2,1)} %bitcast.14, s32[768]{0:T(1024)} %crop_s.1, s32[1,768]{1,0:T(1,128)} %reshape.40.crop_v, bf16[128,128]{1,0:T(8,128)(2,1)} %w_ag.1, bf16[128,128]{1,0:T(8,128)(2,1)} %w_av.1, ...), custom_call_target="tpu_custom_call" | custom-call | tf_op jit(solution)/shard_map/pallas_call | solution.py:678
  168.4 13.4 %shard_map.230 = (bf16[9216,128]{1,0:T(8,128)(2,1)}, bf16[384,96]{1,0:T(8,128)(2,1)}, f32[9216,128]{1,0:T(8,128)}) custom-call(bf16[9216,128]{1,0:T(8,128)(2,1)} %get-tuple-element.9.pair_rows, bf16[384,96]{1,0:T(8,128)(2,1)} %get-tuple-element.10.token_rows, bf16[96,16,128]{2,1,0:T(8,128)(2,1)} %bitcast.15, f32[1,128]{1,0:T(1,128)} %bitcast.25, ...), custom_call_target="tpu_custom_call" | custom-call | tf_op jit(solution)/shard_map/pallas_call | solution.py:694

commit v3 on v2

--- a/solution.py
+++ b/solution.py
@@ -18,6 +18,7 @@
 G = 24
 CH = 8
 RC = 3 * B
+CR = 16 * B + 32
 
 
 def nt(a, b):
@@ -33,14 +34,14 @@
 
 
 def row_means(values, ones):
-    high = values.astype(BF16)
-    low = (values - high.astype(F32)).astype(BF16)
-    return nn(jnp.concatenate([high, low], axis=1), ones)
+    half = values.shape[0] // 2
+    out = nn(jnp.concatenate([values[:half], values[half:]], axis=1), ones)
+    return jnp.concatenate([out[:, :128], out[:, 128:]], axis=0)
 
 
 def centered(values, ones):
-    center = values.astype(F32) - nn(values, ones[0:128])
-    return center, lax.rsqrt(row_means(center * center, ones) + 1e-05)
+    center = values.astype(F32) - row_means(values, ones)
+    return center, lax.rsqrt(row_means((center * center).astype(BF16), ones) + 1e-05)
 
 
 def normalize(values, ones):
@@ -49,7 +50,9 @@
 
 
 def mean_weights():
-    return jnp.full((256, 128), 1.0 / 128.0, BF16)
+    first = lax.broadcasted_iota(jnp.int32, (256, 256), 0) < 128
+    second = lax.broadcasted_iota(jnp.int32, (256, 256), 1) < 128
+    return jnp.where(first == second, 1.0 / 128.0, 0.0).astype(BF16)
 
 
 def kernel(
@@ -57,11 +60,11 @@
     lnb, wpbt, tokens, cot, lnt, wq, wk, wv, wg, wo,
     pair_out, tokens_out, bg,
     wt, w_op, xd, cd,
-    normed, lf, rf, lm, rslab, part, z_recv, y_recv, own_sum, x_send, x_recv, slab, q_s, kslab,
-    vslab, gate_s, datt_s, tri_send, tri_recv, tri_f, hb_f, hb_send, hb, bias, acc, g_send, g_recv,
+    ones_ref, normed, made, lf, rf, lm2, lm1, rslab, part, z_recv, y_recv, own_sum, x_send, x_recv, slab, q_s, kslab,
+    vslab, gate_s, datt_s, tri_send, tri_recv, tri_f, hb_f, hb_send, hb, bias, raw, d_probs, acc, g_send, g_recv,
     pj_send, py_recv, px_own, px_send, px_recv, sg, cg, cg_f,
     slab_ss, slab_rs, ring_ss, ring_rs, z_ss, z_rs, y_ss, y_rs, x_ss, x_rs,
-    k_ss, k_rs, v_ss, v_rs, t_ss, t_rs, h_ss, h_rs, hg_ss, hg_rs, po_ss, po_rs, pr_ss, pr_rs,
+    kv_ss, kv_rs, t_ss, t_rs, h_ss, h_rs, hg_ss, hg_rs, po_ss, po_rs, pr_ss, pr_rs,
     py_ss, py_rs, px_ss, px_rs, g_ss, g_rs, c_ss, c_rs, b_ss, b_rs,
 ):
     row = lax.axis_index("row")
@@ -70,7 +73,8 @@
     xh = col // 4
     yy = col % 4
     xp = (1 - xh) * 4 + yy
-    ones = mean_weights()
+    ones_ref[...] = mean_weights()
+    ones = ones_ref[...]
     right = (row + 1) % NR
     left = (row + NR - 1) % NR
 
@@ -88,8 +92,6 @@
         pl.semaphore_signal(
             barrier, inc=1, device_id={"samp": (samp + d) % NS}, device_id_type=MESH
         )
-
-    pl.semaphore_wait(barrier, NC + NR + NS - 3)
 
     def around(d):
         return (yy + d) % 4
@@ -108,8 +110,6 @@
     ]
     slab[col, 0] = tokens[...]
     slab[col, 1] = cot[...]
-    for c in [slab_x] + slab_own:
-        c.start()
 
     for n, w in enumerate((w_ag, w_av, w_bg, w_bv)):
         wt[n] = w[...].astype(F32).T.astype(BF16)
@@ -118,45 +118,52 @@
     w_op[...] = jnp.concatenate(
         [tri_f[pl.ds(0, 64, stride=2), :], tri_f[pl.ds(1, 64, stride=2), :]], axis=0
     ).astype(BF16)
+    crop = jnp.concatenate([crop_v[i : i + 1, :] for i in range(6)], axis=1).astype(F32)
+    token_gain = jnp.concatenate([lnt[i : i + 1, :] for i in range(6)], axis=1)
     keep_cols = jnp.zeros((1, B), F32)
     for b in range(NC):
-        here = crop_v[0:1, b * B : b * B + B].astype(F32)
-        keep_cols = jnp.where(col == b, here, keep_cols)
+        keep_cols = jnp.where(col == b, crop[:, b * B : b * B + B], keep_cols)
     keep_cols = jnp.concatenate([keep_cols, jnp.zeros((1, 32), F32)], axis=1)
 
-    def norm_step(m, carry):
-        for e in range(4):
-            at = pl.ds(pl.multiple_of(m * 1536 + e * 384, 384), 384)
-            normed[at, :] = (normalize(pair[at, :], ones) * lnp[...]).astype(BF16)
+    for m in range(6):
+        normed[m * CR + 16 * B : m * CR + CR, :] = jnp.zeros((32, 128), BF16)
+    lane = lax.broadcasted_iota(jnp.int32, (8, 128), 1)
+    wide = lane < B
+
+    def norm_chunk(m):
+        src = pl.ds(pl.multiple_of(m * (16 * B), 16 * B), 16 * B)
+        dst = pl.ds(pl.multiple_of(m * CR, 32), 16 * B)
+        normed[dst, :] = (normalize(pair[src, :], ones) * lnp[...]).astype(BF16)
+
+    def edge_chunk(m):
+        made[...] = nt(normed[pl.ds(pl.multiple_of(m * CR, 32), CR), :], wp)
+        for e in range(16):
+            i = m * 16 + e
+            o = made[e * B : e * B + 128, :].T
+            kept = keep_cols * crop_s[row * B + i].astype(F32)
+            for first, dest in ((0, lf), (64, rf)):
+                edge = jax.nn.sigmoid(o[first : first + 32]) * o[first + 32 : first + 64] * kept
+                tail = edge[24:32]
+                for q in range(3):
+                    packed = jnp.where(wide, edge[8 * q : 8 * q + 8], pltpu.roll(tail, 96 - 32 * q, 1))
+                    dest[pl.ds(i + 8 * B * q, 8, stride=B), :] = packed
+
+    norm_chunk(0)
+
+    pl.semaphore_wait(barrier, NC + NR + NS - 3)
+    for c in [slab_x] + slab_own:
+        c.start()
+
+    def front_step(m, carry):
+        edge_chunk(m)
+        norm_chunk(m + 1)
         return carry
 
-    lax.fori_loop(0, 6, norm_step, 0)
+    lax.fori_loop(0, 5, front_step, 0)
+    edge_chunk(5)
     slab_x_in.wait_recv()
     for c in slab_on:
         c.start()
-    normed[B * B : B * B + 32, :] = jnp.zeros((32, 128), BF16)
-    lane = lax.broadcasted_iota(jnp.int32, (8, 128), 1)
-    wide = lane < B
-
-    def edges(weights, dest):
-        def step(m, carry):
-            for e in range(8):
-                i = m * 8 + e
-                rows = normed[pl.ds(pl.multiple_of(i * B, 32), 128), :]
-                o = nt(weights, rows)
-                kept = keep_cols * crop_s[row * B + i].astype(F32)
-                edge = jax.nn.sigmoid(o[0:32]) * o[32:64] * kept
-                tail = edge[24:32]
-                for q in range(3):
-                    packed = jnp.where(
-                        wide, edge[8 * q : 8 * q + 8], pltpu.roll(tail, 96 - 32 * q, 1)
-                    )
-                    dest[pl.ds(i + 8 * B * q, 8, stride=B), :] = packed
-            return carry
-
-        lax.fori_loop(0, B // 8, step, 0)
-
-    edges(wp[64:128], rf)
     own = lax.broadcasted_iota(jnp.int32, (B, 128), 1) < B
     carriers = [(n, k, pl.ds((k * 8 + n) * B, B)) for n in range(CH) for k in range(3)]
     for n, k, at in carriers:
@@ -177,11 +184,18 @@
     for n in range(3):
         for s in range(2):
             rcopy(n, 1, s, False).start()
-    edges(wp[0:64], lf)
+    empty = jnp.zeros((B, 128), BF16)
     for n, k, at in carriers:
         edge = lf[at, :]
-        lm[3 * n + k, 0:B, :] = jnp.where(own, edge, 0.0).astype(BF16)
-        lm[3 * n + k, B : 2 * B, :] = jnp.where(own, 0.0, edge).astype(BF16)
+        mine = jnp.where(own, edge, 0.0).astype(BF16)
+        rest = jnp.where(own, 0.0, edge).astype(BF16)
+        if k < 2:
+            lm2[n, k * B : k * B + B, k * 128 : k * 128 + 128] = mine
+            lm2[n, k * B : k * B + B, (1 - k) * 128 : (1 - k) * 128 + 128] = empty
+            lm2[n, 2 * B : 3 * B, k * 128 : k * 128 + 128] = rest
+        else:
+            lm1[n, 0:B, :] = mine
+            lm1[n, B : 2 * B, :] = rest
 
     def token_step(pair_of):
         at = pl.ds(pair_of * 2 * B, 2 * B)
@@ -198,7 +212,7 @@
         for b in range(NC):
             xd[:, b * B : b * B + B] = x[b] * inv
             cd[:, b * B : b * B + B] = slab[b, 1, at, :].astype(F32)
-        normal = (xd[...] * lnt[...]).astype(BF16)
+        normal = (xd[...] * token_gain).astype(BF16)
         q_s[at, :] = nt(normal, wq[...]).astype(BF16)
         tokens_at = pl.ds(pl.multiple_of(row * B, B), B)
         for w, dest in ((wk, kslab), (wv, vslab)):
@@ -210,26 +224,24 @@
         d = nt(cd[...].astype(BF16), wo[...])
         datt_s[at, :] = (d * gate).astype(BF16)
 
-    def product(n, j):
-        tops, tail = [], None
-        for q in range(3):
-            o = nt(lm[3 * n + q], rslab[n, j, q * B : q * B + 128, :])
-            tops.append(o[0:B])
-            tail = o[B : 2 * B] if tail is None else tail + o[B : 2 * B]
-        for q in range(3):
-            packed = jnp.where(own, tops[q], pltpu.roll(tail, 96 - 32 * q, 1))
-            part[n, j, q * B : q * B + B, :] = packed.astype(BF16)
-
     def products(n, back):
         if back in (0, 4):
-            product(n, (row + back) % NR)
+            blocks = [(row + back) % NR]
         else:
-
-            def one(d, carry):
-                product(n, (row + NR + (2 * d - 1) * back) % NR)
-                return carry
-
-            lax.fori_loop(0, 2, one, 0)
+            blocks = [(row + NR + step * back) % NR for step in (-1, 1)]
+        rights = [
+            jnp.concatenate([rslab[n, j, q * B : q * B + 128, :] for j in blocks], axis=0)
+            for q in range(3)
+        ]
+        two = nt(lm2[n], jnp.concatenate(rights[:2], axis=1))
+        one = nt(lm1[n], rights[2])
+        for e, j in enumerate(blocks):
+            at = slice(e * 128, e * 128 + 128)
+            tops = [two[0:B, at], two[B : 2 * B, at], one[0:B, at]]
+            tail = two[2 * B : 3 * B, at] + one[B : 2 * B, at]
+            for q in range(3):
+                packed = jnp.where(own, tops[q], pltpu.roll(tail, 96 - 32 * q, 1))
+                part[n, j, q * B : q * B + B, :] = packed.astype(BF16)
 
     sides = (xh * 4 + (yy + 1) % 4, xh * 4 + (yy + 3) % 4)
 
@@ -309,10 +321,15 @@
         for d in range(1, NS):
             tcopy(n, d, False).start()
 
-    def kvcopy(slab, ss, rs, d, inward):
-        block = (row + NR - d) % NR if inward else row
-        at = slab.at[:, pl.ds(pl.multiple_of(block * B, B), B), :]
-        return copy(at, at, ss.at[d], rs.at[d], row=(row + d) % NR)
+    def kvcopies(t, s, inward):
+        back = t if inward else t - 1
+        block = (row + NR + step_of[s] * back) % NR
+        rows = pl.ds(pl.multiple_of(block * B, B), B)
+        both = [(0, kslab), (1, vslab)]
+        return [
+            copy(v.at[:, rows, :], v.at[:, rows, :], kv_ss.at[n, s, t - 1], kv_rs.at[n, s, t - 1], row=ring[s])
+            for n, v in (both if t < 4 else both[s : s + 1])
+        ]
 
     for k in range(CH + 7):
         active = [(n, k - n + 1) for n in range(CH)]
@@ -323,10 +340,15 @@
                         rcopy(n, t - 1, s, True).wait_recv()
                     if t < 5 and not (t == 1 and n < 3):
                         rcopy(n, t, s, False).start()
-        if k == CH + 2:
-            for d in range(1, NR):
-                kvcopy(kslab, k_ss, k_rs, d, False).start()
-                kvcopy(vslab, v_ss, v_rs, d, False).start()
+        t = k - CH + 1
+        if 1 <= t <= 5:
+            for s in range(2):
+                if t > 1:
+                    for c in kvcopies(t - 1, s, True):
+                        c.wait_recv()
+                if t < 5:
+                    for c in kvcopies(t, s, False):
+                        c.start()
         for n, t in active:
             if t == 5:
                 products(n, 4)
@@ -380,7 +402,7 @@
         return copy(at, at, pr_ss, pr_rs, samp=sib)
 
 
-    def post_step(m, carry):
+    def post_rows(m):
         cols = []
         for e in range(4):
             i = m * 4 + e
@@ -394,8 +416,10 @@
         t = center * lax.rsqrt(jnp.mean(center * center, axis=0, keepdims=True) + 1e-05)
         proj = tn(t.astype(BF16), w_op[...])
         proj = jnp.concatenate([proj[e * 128 : e * 128 + B] for e in range(4)], axis=0)
-        at = pl.ds(pl.multiple_of((row0 + m * 4) * B, 4 * B), 4 * B)
-        gate = jax.nn.sigmoid(nn(normed[at, :], w_outgate[...]))
+        first = row0 + m * 4
+        at = pl.ds(pl.multiple_of(first * B, 4 * B), 4 * B)
+        norm_at = pl.ds(pl.multiple_of(first // 16 * CR + first % 16 * B, 32), 4 * B)
+        gate = jax.nn.sigmoid(nn(normed[norm_at, :], w_outgate[...]))
         updated = (pair[at, :].astype(F32) + gate * proj).astype(BF16)
         trans_in = normalize(updated, ones).astype(BF16)
         total = updated.astype(F32)
@@ -405,17 +429,21 @@
             hidden = (a * jax.nn.sigmoid(a) * u).astype(BF16)
             total = total + nn(hidden, w_td[n * 256 : n * 256 + 256, :])
         out = total.astype(BF16)
-        pair_out[at, :] = out
-        for k in range(2):
-            pocopy(k, m, False).start()
         bias_in = (normalize(out, ones) * lnb[...]).astype(BF16)
-        o = nt(wpbt[...], bias_in)
-        for e in range(4):
-            hb_f[pl.ds(m * 4 + e, 16, stride=Q), 0:B] = o[:, e * B : e * B + B]
+        return at, out, nt(wpbt[...], bias_in)
+
+    def post_step(m, carry):
+        done = [post_rows(m * 2 + n) for n in range(2)]
+        for n, (at, out, heads) in enumerate(done):
+            pair_out[at, :] = out
+            for e in range(4):
+                hb_f[pl.ds((m * 2 + n) * 4 + e, 16, stride=Q), 0:B] = heads[:, e * B : e * B + B]
+        for n in range(2):
+            for k in range(2):
+                pocopy(k, m * 2 + n, False).start()
         return carry
 
-    lax.fori_loop(0, Q // 4, post_step, 0)
-
+    lax.fori_loop(0, Q // 8, post_step, 0)
     for c in range(NC):
         hb_send[c] = hb_f[c * 48 : c * 48 + 48, :].astype(BF16)
 
@@ -427,6 +455,21 @@
     for d in range(1, NC):
         hcopy(d, False).start()
     hb[col, samp] = hb_send[col]
+
+    feature = lax.broadcasted_iota(jnp.int32, (1, B), 1)
+    head_masks = [(feature < 48).astype(F32), (feature >= 48).astype(F32)]
+    scale = 1.0 / math.sqrt(48)
+
+    def per_head(v):
+        return jnp.concatenate([v * m.astype(BF16) for m in head_masks], axis=0)
+
+    def before_bias(s):
+        at = slice(s * B, s * B + B)
+        raw[s] = nt(per_head(q_s[at, :]), kslab[s]) * scale
+        d_probs[s] = nt(per_head(datt_s[at, :]), vslab[s])
+
+    before_bias(0)
+    before_bias(1)
     for d in range(1, NC):
         hcopy(d, True).wait_recv()
 
@@ -435,42 +478,39 @@
 
     for d in range(1, NS):
         hgcopy(d, False).start()
-    for d in range(1, NR):
-        kvcopy(kslab, k_ss, k_rs, d, True).wait_recv()
-        kvcopy(vslab, v_ss, v_rs, d, True).wait_recv()
+    before_bias(2)
+    before_bias(3)
     for d in range(1, NS):
         hgcopy(d, True).wait_recv()
 
     for b in range(NC):
-        key_mask = (crop_v[0:1, b * B : b * B + B].astype(F32) - 1.0) * 10000.0
+        key_mask = (crop[:, b * B : b * B + B] - 1.0) * 10000.0
         quarters = [hb[b, n].astype(F32) for n in range(NS)]
         for h in range(2):
             whole = jnp.concatenate([v[h * Q : h * Q + Q, 0:B] for v in quarters], axis=0)
             bias[h * B : h * B + B, b * B : b * B + B] = whole + key_mask
     acc[...] = jnp.zeros((2 * B, NC * B), F32)
-    feature = lax.broadcasted_iota(jnp.int32, (1, B), 1)
-    head_masks = [(feature < 48).astype(F32), (feature >= 48).astype(F32)]
-    scale = 1.0 / math.sqrt(48)
-
-    def att_step(s, carry):
+    def att_rows(s):
         at = pl.ds(pl.multiple_of(s * B, B), B)
-        query, datt = q_s[at, :], datt_s[at, :]
-        query = jnp.concatenate([query * m.astype(BF16) for m in head_masks], axis=0)
-        datt = jnp.concatenate([datt * m.astype(BF16) for m in head_masks], axis=0)
-        scores = nt(query, kslab[s]) * scale + bias[...]
+        scores = raw[s] + bias[...]
         shifted = jnp.exp(scores - jnp.max(scores, axis=-1, keepdims=True))
         probs = shifted * (1.0 / jnp.sum(shifted, axis=-1, keepdims=True))
         got = nn(probs.astype(BF16), vslab[s])
-        delta = jnp.sum(datt.astype(F32) * got, axis=-1, keepdims=True)
-        acc[...] = acc[...] + probs * (nt(datt, vslab[s]) - delta)
+        delta = jnp.sum(per_head(datt_s[at, :]).astype(F32) * got, axis=-1, keepdims=True)
         attended = got[0:B] * head_masks[0] + got[B : 2 * B] * head_masks[1]
-        gated = (gate_s[at, :] * attended).astype(BF16)
-        xd[0:B, :] = nn(gated, wo[...])
+        return (gate_s[at, :] * attended).astype(BF16), probs * (d_probs[s] - delta)
+
+    def att_step(m, carry):
+        done = [att_rows(m * 2 + e) for e in range(2)]
+        acc[...] = acc[...] + (done[0][1] + done[1][1])
+        gated = jnp.concatenate([v for v, _ in done], axis=0)
+        at = pl.ds(pl.multiple_of(m * 2 * B, 2 * B), 2 * B)
+        xd[...] = nn(gated, wo[...])
         for b in range(NC):
-            pj_send[b, at, :] = xd[0:B, b * B : b * B + B].astype(BF16)
+            pj_send[b, at, :] = xd[:, b * B : b * B + B].astype(BF16)
         return carry
 
-    lax.fori_loop(0, 4, att_step, 0)
+    lax.fori_loop(0, 2, att_step, 0)
     for m in range(6):
         pocopy(1, m, True).wait_recv()
     prcopy(False).start()
@@ -572,9 +612,10 @@
         for d in range(1, NS):
             tcopy(n, d, False).wait_send()
         xcopy(n).wait_send()
-    for d in range(1, NR):
-        kvcopy(kslab, k_ss, k_rs, d, False).wait_send()
-        kvcopy(vslab, v_ss, v_rs, d, False).wait_send()
+    for t in range(1, 5):
+        for s in range(2):
+            for c in kvcopies(t, s, False):
+                c.wait_send()
     for d in range(1, NC):
         hcopy(d, False).wait_send()
         ccopy(d, False).wait_send()
@@ -601,14 +642,22 @@
     weights = wpbt[...].astype(F32) * lnb[...]
     weights = weights - jnp.mean(weights, axis=-1, keepdims=True)
     weights = jnp.concatenate(split(weights), axis=0)
-    for e in range(2):
+    empty = jnp.zeros((48, 128), BF16)
+    weights = jnp.concatenate(
+        [jnp.concatenate([weights, empty], axis=1), jnp.concatenate([empty, weights], axis=1)], axis=0
+    )
+    for e in range(4):
         at = slice(e * 4 * B, e * 4 * B + 4 * B)
-        grads = jnp.concatenate([bg[e * 4 + i] for i in range(4)], axis=1)
-        scaled = tn(jnp.concatenate([grads, grads, grads], axis=0), weights)
-        scaled = jnp.concatenate([scaled[i * 128 : i * 128 + B] for i in range(4)], axis=0)
+        even, odd = [
+            jnp.concatenate([bg[e * 4 + n], bg[e * 4 + 2 + n]], axis=1) for n in range(2)
+        ]
+        both = tn(jnp.concatenate([even] * 3 + [odd] * 3, axis=0), weights)
+        scaled = jnp.concatenate(
+            [both[0:B, :128], both[0:B, 128:], both[128 : 128 + B, :128], both[128 : 128 + B, 128:]], axis=0
+        )
         center, inv = centered(pair_rows[at, :], ones)
         unit = center * inv
-        pair_grad[at, :] = inv * (scaled - unit * row_means(scaled * unit, ones))
+        pair_grad[at, :] = inv * (scaled - unit * row_means((scaled * unit).astype(BF16), ones))
 
 
 def per_device(
@@ -619,10 +668,10 @@
     wpbt = w_pairbias.T
     lnb = ln_bias.reshape(1, 128)
     args = (
-        pair.reshape(B * B, 128), crop_mask, crop_mask.reshape(1, NC * B),
+        pair.reshape(B * B, 128), crop_mask, crop_mask.reshape(6, 128),
         w_agate, w_aval, w_bgate, w_bval, ln_pair.reshape(1, 128), w_outgate, w_outproj,
         w_trans_gate, w_trans_up, w_trans_down, lnb, wpbt,
-        tokens.reshape(4 * B, B), cotangent.reshape(4 * B, B), ln_token.reshape(1, NC * B),
+        tokens.reshape(4 * B, B), cotangent.reshape(4 * B, B), ln_token.reshape(6, 128),
         w_query.T, w_key.T, w_value.T, w_gate.T, w_output,
     )
     vm = pltpu.VMEM
@@ -632,10 +681,13 @@
         vm((128, 128), BF16),
         vm((2 * B, NC * B), F32),
         vm((2 * B, NC * B), F32),
-        vm((B * B + 32, 128), BF16),
+        vm((256, 256), BF16),
+        vm((6 * CR, 128), BF16),
+        vm((CR, 128), F32),
         vm((G * B, 128), F32),
         vm((G * B, 128), F32),
-        vm((G, 2 * B, 128), BF16),
+        vm((CH, 3 * B, 256), BF16),
+        vm((CH, 2 * B, 128), BF16),
         vm((CH, NR, RC + 32, 128), BF16),
         vm((CH, NR, RC, 128), BF16),
         vm((CH, 2, 2, RC // 2, 128), BF16),
@@ -656,6 +708,8 @@
         vm((NC, 48, 128), BF16),
         vm((NC, NS, 48, 128), BF16),
         vm((2 * B, NC * B), F32),
+        vm((4, 2 * B, NC * B), F32),
+        vm((4, 2 * B, NC * B), F32),
         vm((2 * B, NC * B), F32),
         vm((NS, NC, 48, 128), BF16),
         vm((NS, NC, 48, 128), BF16),
@@ -669,7 +723,7 @@
         vm((16 * Q, 128), F32),
     ]
     sems = [(7,)] * 2 + [(CH, 2, 4)] * 2 + [(CH, 2, 2)] * 4 + [(CH,)] * 2
-    sems += [(8,)] * 4 + [(CH, 4)] * 2 + [(8,)] * 2 + [(4,)] * 2 + [(2, 6)] * 2 + [None] * 2
+    sems += [(2, 2, 4)] * 2 + [(CH, 4)] * 2 + [(8,)] * 2 + [(4,)] * 2 + [(2, 6)] * 2 + [None] * 2
     sems += [(4, 2)] * 2 + [None] * 2 + [(4,)] * 2 + [(8,)] * 2 + [(4,)] * 2
     scratch += [dma if s is None else dma(s) for s in sems]
     spec = pl.BlockSpec(memory_space=pltpu.VMEM)
@@ -689,11 +743,11 @@
             collective_id=0, has_side_effects=True, vmem_limit_bytes=56 * 1024 * 1024
         ),
     )(*args)
-    rows = pl.BlockSpec((8 * B, 128), lambda i: (i, 0))
+    rows = pl.BlockSpec((16 * B, 128), lambda i: (i, 0))
     whole = pl.BlockSpec((4 * B, B), lambda i: (0, 0))
     outs = pl.pallas_call(
         finish,
-        grid=(B // 8,),
+        grid=(B // 16,),
         out_shape=(
             jax.ShapeDtypeStruct((B * B, 128), BF16),
             jax.ShapeDtypeStruct((4 * B, B), BF16),
@@ -702,7 +756,7 @@
         in_specs=[
             rows,
             whole,
-            pl.BlockSpec((8, 16, 128), lambda i: (i, 0, 0)),
+            pl.BlockSpec((16, 16, 128), lambda i: (i, 0, 0)),
             pl.BlockSpec((1, 128), lambda i: (0, 0)),
             pl.BlockSpec((16, 128), lambda i: (0, 0)),
         ],

time: 182 us -> 176 us (0.967)
  Pallas kernels: 179 us -> 175 us
  local copies, waits for them, and re-layouts: 2.53 us -> 0 us
    pallas_call x1, Pallas kernels: 13.4 us -> 10.4 us  [per_device(): pl.pallas_call(finish, grid=(B // 16,), out_shape=(jax.ShapeDtypeStruct((...]
    reshape x2 -> x0, local copies, waits for them, and re-layouts: 2.53 us -> none  [the longest x1 1.27 us: per_device(): ln_token.reshape(1, NC * B)]
where the time goes in v3:
time: 176 us; the launch traced here: 175 us
  Pallas kernels  175 us (99%)
    pallas_call x1, Pallas kernels, per_device(): pl.pallas_call(kernel, out_shape=(jax.ShapeDtypeStruct((B * B, 128), BF16...  164 us
    pallas_call x1, Pallas kernels, per_device(): pl.pallas_call(finish, grid=(B // 16,), out_shape=(jax.ShapeDtypeStruct((...  10.4 us

profile of v3, /device:TPU:1, one launch (start us, length us, event | category | flops | bytes accessed | tf_op | source)
XLA Modules:
  0.0 175.4 jit_solution(3149449806389507874)
XLA Ops:
  0.6 164.3 %shard_map.229 = (bf16[9216,128]{1,0:T(8,128)(2,1)}, bf16[384,96]{1,0:T(8,128)(2,1)}, bf16[4,24,16,128]{3,2,1,0:T(8,128)(2,1)}) custom-call(bf16[9216,128]{1,0:T(8,128)(2,1)} %bitcast.16, s32[768]{0:T(1024)} %crop_s.1, s32[6,128]{1,0:T(8,128)} %bitcast.26, bf16[128,128]{1,0:T(8,128)(2,1)} %w_ag.1, bf16[128,128]{1,0:T(8,128)(2,1)} %w_av.1, ...), custom_call_target="tpu_custom_call" | custom-call | tf_op jit(solution)/shard_map/pallas_call | solution.py:732
  164.9 10.4 %shard_map.230 = (bf16[9216,128]{1,0:T(8,128)(2,1)}, bf16[384,96]{1,0:T(8,128)(2,1)}, f32[9216,128]{1,0:T(8,128)}) custom-call(bf16[9216,128]{1,0:T(8,128)(2,1)} %get-tuple-element.9.pair_rows, bf16[384,96]{1,0:T(8,128)(2,1)} %get-tuple-element.10.token_rows, bf16[96,16,128]{2,1,0:T(8,128)(2,1)} %bitcast.17, f32[1,128]{1,0:T(1,128)} %bitcast.29, ...), custom_call_target="tpu_custom_call" | custom-call | tf_op jit(solution)/shard_map/pallas_call | solution.py:748

commit v4 on v3

--- a/solution.py
+++ b/solution.py
@@ -241,43 +241,47 @@
             tail = two[2 * B : 3 * B, at] + one[B : 2 * B, at]
             for q in range(3):
                 packed = jnp.where(own, tops[q], pltpu.roll(tail, 96 - 32 * q, 1))
-                part[n, j, q * B : q * B + B, :] = packed.astype(BF16)
+                part[n, j % 4, j // 4, q * B : q * B + B, :] = packed.astype(BF16)
 
     sides = (xh * 4 + (yy + 1) % 4, xh * 4 + (yy + 3) % 4)
 
-    def zcopy(n, s, x):
-        src = part.at[n, x * 4 + (yy + 2) % 4, pl.ds(s * (RC // 2), RC // 2)]
-        return copy(src, z_recv.at[n, s, x], z_ss.at[n, s, x], z_rs.at[n, s, x], col=sides[s])
-
-    def ycopy(n, s, x):
-        src = part.at[n, x * 4 + (yy + 1 + 2 * s) % 4]
-        return copy(src, y_recv.at[n, s, x], y_ss.at[n, s, x], y_rs.at[n, s, x], col=sides[s])
-
-    each = [(s, x) for s in range(2) for x in range(2)]
+    def zcopy(n, s):
+        src = part.at[n, (yy + 2) % 4, :, pl.ds(s * (RC // 2), RC // 2)]
+        return copy(src, z_recv.at[n, s], z_ss.at[n, s], z_rs.at[n, s], col=sides[s])
+
+    def ycopy(n, s):
+        there = (yy + (1, 3, 2)[s]) % 4
+        return copy(
+            part.at[n, there], y_recv.at[n, s], y_ss.at[n, s], y_rs.at[n, s], col=xh * 4 + there
+        )
+
+    def y_ways(n):
+        return (0, 1, 2) if n >= CH - 2 else (0, 1)
 
     def z_start(n):
-        for s, x in each:
-            zcopy(n, s, x).start()
+        for s in range(2):
+            zcopy(n, s).start()
 
     def y_start(n):
-        for s, x in each:
-            zcopy(n, s, x).wait_recv()
-            j = x * 4 + (yy + 1 + 2 * s) % 4
-            at = pl.ds(s * (RC // 2), RC // 2)
-            more = z_recv[n, s, x].astype(F32)
-            part[n, j, at, :] = (part[n, j, at, :].astype(F32) + more).astype(BF16)
-            ycopy(n, s, x).start()
+        for s in range(2):
+            zcopy(n, s).wait_recv()
+            for x in range(2):
+                at = pl.ds(s * (RC // 2), RC // 2)
+                more = z_recv[n, s, x].astype(F32)
+                there = (yy + 1 + 2 * s) % 4
+                part[n, there, x, at, :] = (part[n, there, x, at, :].astype(F32) + more).astype(BF16)
+            ycopy(n, s).start()
 
     def y_sum(n):
-        for s, x in each:
-            ycopy(n, s, x).wait_recv()
+        for s in y_ways(n):
+            ycopy(n, s).wait_recv()
 
         def one(k, carry):
             at = pl.ds(pl.multiple_of(k * B, B), B)
 
             def total(x):
-                v = part[n, x * 4 + yy, at, :].astype(F32)
-                for s in range(2):
+                v = part[n, yy, x, at, :].astype(F32)
+                for s in y_ways(n):
                     v = v + y_recv[n, s, x, at, :].astype(F32)
                 return v
 
@@ -331,7 +335,7 @@
             for n, v in (both if t < 4 else both[s : s + 1])
         ]
 
-    for k in range(CH + 7):
+    for k in range(CH + 6):
         active = [(n, k - n + 1) for n in range(CH)]
         for n, t in active:
             if 1 <= t <= 5:
@@ -350,23 +354,28 @@
                     for c in kvcopies(t, s, False):
                         c.start()
         for n, t in active:
+            straight = n >= CH - 2
             if t == 5:
                 products(n, 4)
-                z_start(n)
-            elif t == 6:
+                if straight:
+                    for s in y_ways(n):
+                        ycopy(n, s).start()
+                else:
+                    z_start(n)
+            elif t == 6 and not straight:
                 y_start(n)
-            elif t == 7:
+            elif t == 7 - straight:
                 y_sum(n)
-            elif t == 8:
+            elif t == 8 - straight:
                 triangle(n)
         for n, t in active:
             if 1 <= t <= 4:
                 products(n, t - 1)
-        if k == 1:
+        if k == 4:
             for c in slab_own_in + slab_on_in:
                 c.wait_recv()
-        if k in (1, 3):
-            token_step(k // 2)
+        if k in (4, 6):
+            token_step(k // 2 - 2)
 
     def unpack(m):
         for n in range(CH):
@@ -606,9 +615,11 @@
         for s in range(2):
             for t in range(1, 5):
                 rcopy(n, t, s, False).wait_send()
-        for s, x in each:
-            zcopy(n, s, x).wait_send()
-            ycopy(n, s, x).wait_send()
+        for s in y_ways(n):
+            ycopy(n, s).wait_send()
+        if n < CH - 2:
+            for s in range(2):
+                zcopy(n, s).wait_send()
         for d in range(1, NS):
             tcopy(n, d, False).wait_send()
         xcopy(n).wait_send()
@@ -689,9 +700,9 @@
         vm((CH, 3 * B, 256), BF16),
         vm((CH, 2 * B, 128), BF16),
         vm((CH, NR, RC + 32, 128), BF16),
-        vm((CH, NR, RC, 128), BF16),
+        vm((CH, 4, 2, RC, 128), BF16),
         vm((CH, 2, 2, RC // 2, 128), BF16),
-        vm((CH, 2, 2, RC, 128), BF16),
+        vm((CH, 3, 2, RC, 128), BF16),
         vm((CH, RC, 128), F32),
         vm((CH, RC, 128), BF16),
         vm((CH, RC, 128), BF16),
@@ -722,7 +733,7 @@
         vm((NC, 48, 128), BF16),
         vm((16 * Q, 128), F32),
     ]
-    sems = [(7,)] * 2 + [(CH, 2, 4)] * 2 + [(CH, 2, 2)] * 4 + [(CH,)] * 2
+    sems = [(7,)] * 2 + [(CH, 2, 4)] * 2 + [(CH, 2)] * 2 + [(CH, 3)] * 2 + [(CH,)] * 2
     sems += [(2, 2, 4)] * 2 + [(CH, 4)] * 2 + [(8,)] * 2 + [(4,)] * 2 + [(2, 6)] * 2 + [None] * 2
     sems += [(4, 2)] * 2 + [None] * 2 + [(4,)] * 2 + [(8,)] * 2 + [(4,)] * 2
     scratch += [dma if s is None else dma(s) for s in sems]

time: 176 us -> 171 us (0.972)
  Pallas kernels: 175 us -> 170 us
    pallas_call x1, Pallas kernels: 164 us -> 160 us  [per_device(): pl.pallas_call(kernel, out_shape=(jax.ShapeDtypeStruct((B * B, 128), BF16...]
where the time goes in v4:
time: 171 us
  Pallas kernels  170 us (99%)
    pallas_call x1, Pallas kernels, per_device(): pl.pallas_call(kernel, out_shape=(jax.ShapeDtypeStruct((B * B, 128), BF16...  160 us
    pallas_call x1, Pallas kernels, per_device(): pl.pallas_call(finish, grid=(B // 16,), out_shape=(jax.ShapeDtypeStruct((...  10.4 us

profile of v4, /device:TPU:1, one launch (start us, length us, event | category | flops | bytes accessed | tf_op | source)
XLA Modules:
  0.0 170.6 jit_solution(15858417976772684396)
XLA Ops:
  0.6 159.5 %shard_map.229 = (bf16[9216,128]{1,0:T(8,128)(2,1)}, bf16[384,96]{1,0:T(8,128)(2,1)}, bf16[4,24,16,128]{3,2,1,0:T(8,128)(2,1)}) custom-call(bf16[9216,128]{1,0:T(8,128)(2,1)} %bitcast.16, s32[768]{0:T(1024)} %crop_s.1, s32[6,128]{1,0:T(8,128)} %bitcast.26, bf16[128,128]{1,0:T(8,128)(2,1)} %w_ag.1, bf16[128,128]{1,0:T(8,128)(2,1)} %w_av.1, ...), custom_call_target="tpu_custom_call" | custom-call | tf_op jit(solution)/shard_map/pallas_call | solution.py:743
  160.2 10.4 %shard_map.230 = (bf16[9216,128]{1,0:T(8,128)(2,1)}, bf16[384,96]{1,0:T(8,128)(2,1)}, f32[9216,128]{1,0:T(8,128)}) custom-call(bf16[9216,128]{1,0:T(8,128)(2,1)} %get-tuple-element.9.pair_rows, bf16[384,96]{1,0:T(8,128)(2,1)} %get-tuple-element.10.token_rows, bf16[96,16,128]{2,1,0:T(8,128)(2,1)} %bitcast.17, f32[1,128]{1,0:T(1,128)} %bitcast.29, ...), custom_call_target="tpu_custom_call" | custom-call | tf_op jit(solution)/shard_map/pallas_call | solution.py:759

commit v5 on v4

--- a/solution.py
+++ b/solution.py
@@ -197,7 +197,7 @@
             lm1[n, 0:B, :] = mine
             lm1[n, B : 2 * B, :] = rest
 
-    def token_step(pair_of):
+    def token_rows(pair_of):
         at = pl.ds(pair_of * 2 * B, 2 * B)
         x = [slab[b, 0, at, :].astype(F32) for b in range(NC)]
         total = x[0]
@@ -212,13 +212,19 @@
         for b in range(NC):
             xd[:, b * B : b * B + B] = x[b] * inv
             cd[:, b * B : b * B + B] = slab[b, 1, at, :].astype(F32)
+
+    def token_keys(pair_of):
         normal = (xd[...] * token_gain).astype(BF16)
-        q_s[at, :] = nt(normal, wq[...]).astype(BF16)
         tokens_at = pl.ds(pl.multiple_of(row * B, B), B)
         for w, dest in ((wk, kslab), (wv, vslab)):
             out = nt(normal, w[...]).astype(BF16)
             for e in range(2):
                 dest[pair_of * 2 + e, tokens_at, :] = out[e * B : e * B + B]
+
+    def token_queries(pair_of):
+        at = pl.ds(pair_of * 2 * B, 2 * B)
+        normal = (xd[...] * token_gain).astype(BF16)
+        q_s[at, :] = nt(normal, wq[...]).astype(BF16)
         gate = jax.nn.sigmoid(nt(normal, wg[...]))
         gate_s[at, :] = gate
         d = nt(cd[...].astype(BF16), wo[...])
@@ -335,47 +341,56 @@
             for n, v in (both if t < 4 else both[s : s + 1])
         ]
 
+    def ring_slot(n, t):
+        for s in range(2):
+            if t > 1:
+                rcopy(n, t - 1, s, True).wait_recv()
+            if t < 5 and not (t == 1 and n < 3):
+                rcopy(n, t, s, False).start()
+        products(n, t - 1)
+        if t == 5 and n >= CH - 2:
+            for s in y_ways(n):
+                ycopy(n, s).start()
+        elif t == 5:
+            z_start(n)
+
+    def kv_slot(t):
+        for s in range(2):
+            if t > 1:
+                for c in kvcopies(t - 1, s, True):
+                    c.wait_recv()
+            if t < 5:
+                for c in kvcopies(t, s, False):
+                    c.start()
+
+    def token_wait(_):
+        for c in slab_own_in + slab_on_in:
+            c.wait_recv()
+
     for k in range(CH + 6):
-        active = [(n, k - n + 1) for n in range(CH)]
-        for n, t in active:
-            if 1 <= t <= 5:
-                for s in range(2):
-                    if t > 1:
-                        rcopy(n, t - 1, s, True).wait_recv()
-                    if t < 5 and not (t == 1 and n < 3):
-                        rcopy(n, t, s, False).start()
-        t = k - CH + 1
-        if 1 <= t <= 5:
-            for s in range(2):
-                if t > 1:
-                    for c in kvcopies(t - 1, s, True):
-                        c.wait_recv()
-                if t < 5:
-                    for c in kvcopies(t, s, False):
-                        c.start()
-        for n, t in active:
-            straight = n >= CH - 2
-            if t == 5:
-                products(n, 4)
-                if straight:
-                    for s in y_ways(n):
-                        ycopy(n, s).start()
-                else:
-                    z_start(n)
-            elif t == 6 and not straight:
-                y_start(n)
-            elif t == 7 - straight:
-                y_sum(n)
-            elif t == 8 - straight:
-                triangle(n)
-        for n, t in active:
-            if 1 <= t <= 4:
-                products(n, t - 1)
+        between = []
+        for n in range(CH):
+            t = k - n + 1 + (n >= CH - 2)
+            if t == 8:
+                between.append((triangle, n))
+            elif t == 7:
+                between.append((y_sum, n))
+            elif t == 6 and n < CH - 2:
+                between.append((y_start, n))
         if k == 4:
-            for c in slab_own_in + slab_on_in:
-                c.wait_recv()
-        if k in (4, 6):
-            token_step(k // 2 - 2)
+            between.append((token_wait, 0))
+        if k in (4, 5):
+            between += [(f, k - 4) for f in (token_rows, token_keys, token_queries)]
+        for n in range(CH):
+            if 1 <= k - n + 1 <= 5:
+                ring_slot(n, k - n + 1)
+                if between:
+                    f, arg = between.pop(0)
+                    f(arg)
+        if 1 <= k - CH + 1 <= 5:
+            kv_slot(k - CH + 1)
+        for f, arg in between:
+            f(arg)
 
     def unpack(m):
         for n in range(CH):

time: 171 us -> 163 us (0.953)
  Pallas kernels: 170 us -> 162 us
    pallas_call x1, Pallas kernels: 160 us -> 151 us  [per_device(): pl.pallas_call(kernel, out_shape=(jax.ShapeDtypeStruct((B * B, 128), BF16...]
where the time goes in v5:
time: 163 us; the launch traced here: 162 us
  Pallas kernels  162 us (99%)
    pallas_call x1, Pallas kernels, per_device(): pl.pallas_call(kernel, out_shape=(jax.ShapeDtypeStruct((B * B, 128), BF16...  151 us
    pallas_call x1, Pallas kernels, per_device(): pl.pallas_call(finish, grid=(B // 16,), out_shape=(jax.ShapeDtypeStruct((...  10.4 us

profile of v5, /device:TPU:1, one launch (start us, length us, event | category | flops | bytes accessed | tf_op | source)
XLA Modules:
  0.0 162.5 jit_solution(766045005197400497)
XLA Ops:
  0.6 151.4 %shard_map.229 = (bf16[9216,128]{1,0:T(8,128)(2,1)}, bf16[384,96]{1,0:T(8,128)(2,1)}, bf16[4,24,16,128]{3,2,1,0:T(8,128)(2,1)}) custom-call(bf16[9216,128]{1,0:T(8,128)(2,1)} %bitcast.16, s32[768]{0:T(1024)} %crop_s.1, s32[6,128]{1,0:T(8,128)} %bitcast.26, bf16[128,128]{1,0:T(8,128)(2,1)} %w_ag.1, bf16[128,128]{1,0:T(8,128)(2,1)} %w_av.1, ...), custom_call_target="tpu_custom_call" | custom-call | tf_op jit(solution)/shard_map/pallas_call | solution.py:758
  152.1 10.4 %shard_map.230 = (bf16[9216,128]{1,0:T(8,128)(2,1)}, bf16[384,96]{1,0:T(8,128)(2,1)}, f32[9216,128]{1,0:T(8,128)}) custom-call(bf16[9216,128]{1,0:T(8,128)(2,1)} %get-tuple-element.9.pair_rows, bf16[384,96]{1,0:T(8,128)(2,1)} %get-tuple-element.10.token_rows, bf16[96,16,128]{2,1,0:T(8,128)(2,1)} %bitcast.17, f32[1,128]{1,0:T(1,128)} %bitcast.29, ...), custom_call_target="tpu_custom_call" | custom-call | tf_op jit(solution)/shard_map/pallas_call | solution.py:774

commit v6 on v5

--- a/solution.py
+++ b/solution.py
@@ -18,7 +18,7 @@
 G = 24
 CH = 8
 RC = 3 * B
-CR = 16 * B + 32
+CR = 16 * B
 
 
 def nt(a, b):
@@ -60,7 +60,7 @@
     lnb, wpbt, tokens, cot, lnt, wq, wk, wv, wg, wo,
     pair_out, tokens_out, bg,
     wt, w_op, xd, cd,
-    ones_ref, normed, made, lf, rf, lm2, lm1, rslab, part, z_recv, y_recv, own_sum, x_send, x_recv, slab, q_s, kslab,
+    ones_ref, normed, made, lf, rf, lm, rslab, part, z_recv, y_recv, own_sum, x_send, x_recv, slab, q_s, kslab,
     vslab, gate_s, datt_s, tri_send, tri_recv, tri_f, hb_f, hb_send, hb, bias, raw, d_probs, acc, g_send, g_recv,
     pj_send, py_recv, px_own, px_send, px_recv, sg, cg, cg_f,
     slab_ss, slab_rs, ring_ss, ring_rs, z_ss, z_rs, y_ss, y_rs, x_ss, x_rs,
@@ -120,13 +120,16 @@
     ).astype(BF16)
     crop = jnp.concatenate([crop_v[i : i + 1, :] for i in range(6)], axis=1).astype(F32)
     token_gain = jnp.concatenate([lnt[i : i + 1, :] for i in range(6)], axis=1)
-    keep_cols = jnp.zeros((1, B), F32)
-    for b in range(NC):
-        keep_cols = jnp.where(col == b, crop[:, b * B : b * B + B], keep_cols)
-    keep_cols = jnp.concatenate([keep_cols, jnp.zeros((1, 32), F32)], axis=1)
-
-    for m in range(6):
-        normed[m * CR + 16 * B : m * CR + CR, :] = jnp.zeros((32, 128), BF16)
+
+    def keep_lanes(block):
+        kept = jnp.zeros((1, B), F32)
+        for b in range(NC):
+            kept = jnp.where(block == b, crop[:, b * B : b * B + B], kept)
+        return jnp.concatenate([kept, jnp.zeros((1, 32), F32)], axis=1)
+
+    keep_rows, keep_cols = keep_lanes(row), keep_lanes(col)
+
+    made[B * B : B * B + 32, :] = jnp.zeros((32, 128), F32)
     lane = lax.broadcasted_iota(jnp.int32, (8, 128), 1)
     wide = lane < B
 
@@ -135,18 +138,31 @@
         dst = pl.ds(pl.multiple_of(m * CR, 32), 16 * B)
         normed[dst, :] = (normalize(pair[src, :], ones) * lnp[...]).astype(BF16)
 
-    def edge_chunk(m):
-        made[...] = nt(normed[pl.ds(pl.multiple_of(m * CR, 32), CR), :], wp)
-        for e in range(16):
-            i = m * 16 + e
-            o = made[e * B : e * B + 128, :].T
-            kept = keep_cols * crop_s[row * B + i].astype(F32)
-            for first, dest in ((0, lf), (64, rf)):
-                edge = jax.nn.sigmoid(o[first : first + 32]) * o[first + 32 : first + 64] * kept
-                tail = edge[24:32]
-                for q in range(3):
-                    packed = jnp.where(wide, edge[8 * q : 8 * q + 8], pltpu.roll(tail, 96 - 32 * q, 1))
-                    dest[pl.ds(i + 8 * B * q, 8, stride=B), :] = packed
+    def made_chunk(m):
+        at = pl.ds(pl.multiple_of(m * CR, CR), CR)
+        made[at, :] = nt(normed[at, :], wp)
+
+    def edge(o, first, kept):
+        return jax.nn.sigmoid(o[first : first + 32]) * o[first + 32 : first + 64] * kept
+
+    def right_step(m, carry):
+        for e in range(8):
+            k = m * 8 + e
+            rows = jnp.concatenate([made[pl.ds(k, B, stride=B), :], jnp.zeros((32, 128), F32)], axis=0)
+            v = edge(rows.T, 64, keep_rows * crop_s[col * B + k].astype(F32))
+            for q in range(3):
+                packed = jnp.where(wide, v[8 * q : 8 * q + 8], pltpu.roll(v[24:32], 96 - 32 * q, 1))
+                rf[pl.ds(k + 8 * B * q, 8, stride=B), :] = packed
+        return carry
+
+    def left_step(m, carry):
+        for e in range(8):
+            i = m * 8 + e
+            rows = made[pl.ds(pl.multiple_of(i * B, B), 128), :]
+            v = edge(rows.T, 0, keep_cols * crop_s[row * B + i].astype(F32))
+            for q in range(4):
+                lf[pl.ds(i + 8 * B * q, 8, stride=B), :] = v[8 * q : 8 * q + 8]
+        return carry
 
     norm_chunk(0)
 
@@ -155,12 +171,13 @@
         c.start()
 
     def front_step(m, carry):
-        edge_chunk(m)
+        made_chunk(m)
         norm_chunk(m + 1)
         return carry
 
     lax.fori_loop(0, 5, front_step, 0)
-    edge_chunk(5)
+    made_chunk(5)
+    lax.fori_loop(0, B // 8, right_step, 0)
     slab_x_in.wait_recv()
     for c in slab_on:
         c.start()
@@ -168,8 +185,6 @@
     carriers = [(n, k, pl.ds((k * 8 + n) * B, B)) for n in range(CH) for k in range(3)]
     for n, k, at in carriers:
         rslab[n, row, k * B : k * B + B, :] = rf[at, :].astype(BF16)
-    for n in range(CH):
-        rslab[n, :, RC : RC + 32, :] = jnp.zeros((NR, 32, 128), BF16)
 
     ring = (right, left)
     step_of = (-1, 1)
@@ -184,18 +199,11 @@
     for n in range(3):
         for s in range(2):
             rcopy(n, 1, s, False).start()
-    empty = jnp.zeros((B, 128), BF16)
-    for n, k, at in carriers:
-        edge = lf[at, :]
-        mine = jnp.where(own, edge, 0.0).astype(BF16)
-        rest = jnp.where(own, 0.0, edge).astype(BF16)
-        if k < 2:
-            lm2[n, k * B : k * B + B, k * 128 : k * 128 + 128] = mine
-            lm2[n, k * B : k * B + B, (1 - k) * 128 : (1 - k) * 128 + 128] = empty
-            lm2[n, 2 * B : 3 * B, k * 128 : k * 128 + 128] = rest
-        else:
-            lm1[n, 0:B, :] = mine
-            lm1[n, B : 2 * B, :] = rest
+    lax.fori_loop(0, B // 8, left_step, 0)
+    for n in range(CH):
+        for q in range(3):
+            for half, c in enumerate((q * 8 + n, 24 + n)):
+                lm[n, q, half * B : half * B + B, :] = lf[c * B : c * B + B, 0:B].astype(BF16)
 
     def token_rows(pair_of):
         at = pl.ds(pair_of * 2 * B, 2 * B)
@@ -235,19 +243,13 @@
             blocks = [(row + back) % NR]
         else:
             blocks = [(row + NR + step * back) % NR for step in (-1, 1)]
-        rights = [
-            jnp.concatenate([rslab[n, j, q * B : q * B + 128, :] for j in blocks], axis=0)
-            for q in range(3)
-        ]
-        two = nt(lm2[n], jnp.concatenate(rights[:2], axis=1))
-        one = nt(lm1[n], rights[2])
-        for e, j in enumerate(blocks):
-            at = slice(e * 128, e * 128 + 128)
-            tops = [two[0:B, at], two[B : 2 * B, at], one[0:B, at]]
-            tail = two[2 * B : 3 * B, at] + one[B : 2 * B, at]
-            for q in range(3):
-                packed = jnp.where(own, tops[q], pltpu.roll(tail, 96 - 32 * q, 1))
-                part[n, j % 4, j // 4, q * B : q * B + B, :] = packed.astype(BF16)
+        for q in range(3):
+            rights = [rslab[n, j, q * B : q * B + B, :] for j in blocks]
+            o = nn(lm[n, q], jnp.concatenate(rights, axis=1))
+            for e, j in enumerate(blocks):
+                at = slice(e * 128, e * 128 + 128)
+                packed = jnp.where(own, o[0:B, at], o[B : 2 * B, at]).astype(BF16)
+                part[n, j % 4, j // 4, q * B : q * B + B, :] = packed
 
     sides = (xh * 4 + (yy + 1) % 4, xh * 4 + (yy + 3) % 4)
 
@@ -709,12 +711,11 @@
         vm((2 * B, NC * B), F32),
         vm((256, 256), BF16),
         vm((6 * CR, 128), BF16),
-        vm((CR, 128), F32),
+        vm((B * B + 32, 128), F32),
+        vm((32 * B, 128), F32),
         vm((G * B, 128), F32),
-        vm((G * B, 128), F32),
-        vm((CH, 3 * B, 256), BF16),
-        vm((CH, 2 * B, 128), BF16),
-        vm((CH, NR, RC + 32, 128), BF16),
+        vm((CH, 3, 2 * B, B), BF16),
+        vm((CH, NR, RC, 128), BF16),
         vm((CH, 4, 2, RC, 128), BF16),
         vm((CH, 2, 2, RC // 2, 128), BF16),
         vm((CH, 3, 2, RC, 128), BF16),

time: 163 us -> 164 us (level)
  Pallas kernels: 162 us -> 164 us
    pallas_call x1, Pallas kernels: 151 us -> 153 us  [per_device(): pl.pallas_call(kernel, out_shape=(jax.ShapeDtypeStruct((B * B, 128), BF16...]
where the time goes in v6:
time: 164 us
  Pallas kernels  164 us (100%)
    pallas_call x1, Pallas kernels, per_device(): pl.pallas_call(kernel, out_shape=(jax.ShapeDtypeStruct((B * B, 128), BF16...  153 us
    pallas_call x1, Pallas kernels, per_device(): pl.pallas_call(finish, grid=(B // 16,), out_shape=(jax.ShapeDtypeStruct((...  10.4 us

profile of v6, /device:TPU:1, one launch (start us, length us, event | category | flops | bytes accessed | tf_op | source)
XLA Modules:
  0.0 164.3 jit_solution(12507855408977576885)
XLA Ops:
  0.6 153.2 %shard_map.229 = (bf16[9216,128]{1,0:T(8,128)(2,1)}, bf16[384,96]{1,0:T(8,128)(2,1)}, bf16[4,24,16,128]{3,2,1,0:T(8,128)(2,1)}) custom-call(bf16[9216,128]{1,0:T(8,128)(2,1)} %bitcast.16, s32[768]{0:T(1024)} %crop_s.1, s32[6,128]{1,0:T(8,128)} %bitcast.26, bf16[128,128]{1,0:T(8,128)(2,1)} %w_ag.1, bf16[128,128]{1,0:T(8,128)(2,1)} %w_av.1, ...), custom_call_target="tpu_custom_call" | custom-call | tf_op jit(solution)/shard_map/pallas_call | solution.py:759
  153.8 10.4 %shard_map.230 = (bf16[9216,128]{1,0:T(8,128)(2,1)}, bf16[384,96]{1,0:T(8,128)(2,1)}, f32[9216,128]{1,0:T(8,128)}) custom-call(bf16[9216,128]{1,0:T(8,128)(2,1)} %get-tuple-element.9.pair_rows, bf16[384,96]{1,0:T(8,128)(2,1)} %get-tuple-element.10.token_rows, bf16[96,16,128]{2,1,0:T(8,128)(2,1)} %bitcast.17, f32[1,128]{1,0:T(1,128)} %bitcast.29, ...), custom_call_target="tpu_custom_call" | custom-call | tf_op jit(solution)/shard_map/pallas_call | solution.py:775

commit v7 on v6

--- a/solution.py
+++ b/solution.py
@@ -18,6 +18,7 @@
 G = 24
 CH = 8
 RC = 3 * B
+EARLY = 5
 CR = 16 * B
 
 
@@ -196,7 +197,7 @@
         at = rslab.at[n, block, rows]
         return copy(at, at, ring_ss.at[n, s, t - 1], ring_rs.at[n, s, t - 1], row=ring[s])
 
-    for n in range(3):
+    for n in range(EARLY):
         for s in range(2):
             rcopy(n, 1, s, False).start()
     lax.fori_loop(0, B // 8, left_step, 0)
@@ -347,7 +348,7 @@
         for s in range(2):
             if t > 1:
                 rcopy(n, t - 1, s, True).wait_recv()
-            if t < 5 and not (t == 1 and n < 3):
+            if t < 5 and not (t == 1 and n < EARLY):
                 rcopy(n, t, s, False).start()
         products(n, t - 1)
         if t == 5 and n >= CH - 2:
@@ -389,8 +390,8 @@
                 if between:
                     f, arg = between.pop(0)
                     f(arg)
-        if 1 <= k - CH + 1 <= 5:
-            kv_slot(k - CH + 1)
+        if k == CH + 2:
+            kv_slot(1)
         for f, arg in between:
             f(arg)
 
@@ -403,12 +404,14 @@
                     r0 = pl.multiple_of(m * 768, 768) + c // 2 * 48 + c % 2 * Q
                     tri_f[pl.ds(r0, Q), :] = both[e * Q : e * Q + Q]
 
+    kv_slot(2)
     tri_recv[samp] = tri_send[samp]
     unpack(samp)
     for d in range(1, NS):
         for n in range(CH):
             tcopy(n, d, True).wait_recv()
         unpack((samp + NS - d) % NS)
+    kv_slot(3)
 
     row0 = samp * Q
     sib, oth = samp + 1 - 2 * (samp % 2), (samp + 2) % NS
@@ -458,18 +461,19 @@
         bias_in = (normalize(out, ones) * lnb[...]).astype(BF16)
         return at, out, nt(wpbt[...], bias_in)
 
-    def post_step(m, carry):
+    for m in range(3):
         done = [post_rows(m * 2 + n) for n in range(2)]
         for n, (at, out, heads) in enumerate(done):
             pair_out[at, :] = out
             for e in range(4):
                 hb_f[pl.ds((m * 2 + n) * 4 + e, 16, stride=Q), 0:B] = heads[:, e * B : e * B + B]
-        for n in range(2):
-            for k in range(2):
-                pocopy(k, m * 2 + n, False).start()
-        return carry
-
-    lax.fori_loop(0, Q // 8, post_step, 0)
+        if m < 2:
+            for n in range(2):
+                pocopy(0, m * 2 + n, False).start()
+                pocopy(1, m * 2 + n, False).start()
+        if m == 1:
+            kv_slot(4)
+
     for c in range(NC):
         hb_send[c] = hb_f[c * 48 : c * 48 + 48, :].astype(BF16)
 
@@ -494,6 +498,7 @@
         raw[s] = nt(per_head(q_s[at, :]), kslab[s]) * scale
         d_probs[s] = nt(per_head(datt_s[at, :]), vslab[s])
 
+    kv_slot(5)
     before_bias(0)
     before_bias(1)
     for d in range(1, NC):
@@ -504,6 +509,9 @@
 
     for d in range(1, NS):
         hgcopy(d, False).start()
+    for n in range(4, 6):
+        pocopy(0, n, False).start()
+        pocopy(1, n, False).start()
     before_bias(2)
     before_bias(3)
     for d in range(1, NS):

time: 164 us -> 161 us (0.982)
  Pallas kernels: 164 us -> 160 us
    pallas_call x1, Pallas kernels: 153 us -> 150 us  [per_device(): pl.pallas_call(kernel, out_shape=(jax.ShapeDtypeStruct((B * B, 128), BF16...]
where the time goes in v7:
time: 161 us
  Pallas kernels  160 us (99%)
    pallas_call x1, Pallas kernels, per_device(): pl.pallas_call(kernel, out_shape=(jax.ShapeDtypeStruct((B * B, 128), BF16...  150 us
    pallas_call x1, Pallas kernels, per_device(): pl.pallas_call(finish, grid=(B // 16,), out_shape=(jax.ShapeDtypeStruct((...  10.4 us

profile of v7, /device:TPU:1, one launch (start us, length us, event | category | flops | bytes accessed | tf_op | source)
XLA Modules:
  0.0 160.8 jit_solution(4518314344503412453)
XLA Ops:
  0.6 149.7 %shard_map.229 = (bf16[9216,128]{1,0:T(8,128)(2,1)}, bf16[384,96]{1,0:T(8,128)(2,1)}, bf16[4,24,16,128]{3,2,1,0:T(8,128)(2,1)}) custom-call(bf16[9216,128]{1,0:T(8,128)(2,1)} %bitcast.16, s32[768]{0:T(1024)} %crop_s.1, s32[6,128]{1,0:T(8,128)} %bitcast.26, bf16[128,128]{1,0:T(8,128)(2,1)} %w_ag.1, bf16[128,128]{1,0:T(8,128)(2,1)} %w_av.1, ...), custom_call_target="tpu_custom_call" | custom-call | tf_op jit(solution)/shard_map/pallas_call | solution.py:767
  150.3 10.4 %shard_map.230 = (bf16[9216,128]{1,0:T(8,128)(2,1)}, bf16[384,96]{1,0:T(8,128)(2,1)}, f32[9216,128]{1,0:T(8,128)}) custom-call(bf16[9216,128]{1,0:T(8,128)(2,1)} %get-tuple-element.9.pair_rows, bf16[384,96]{1,0:T(8,128)(2,1)} %get-tuple-element.10.token_rows, bf16[96,16,128]{2,1,0:T(8,128)(2,1)} %bitcast.17, f32[1,128]{1,0:T(1,128)} %bitcast.29, ...), custom_call_target="tpu_custom_call" | custom-call | tf_op jit(solution)/shard_map/pallas_call | solution.py:783

commit v8 on v7

--- a/solution.py
+++ b/solution.py
@@ -41,7 +41,8 @@
 
 
 def centered(values, ones):
-    center = values.astype(F32) - row_means(values, ones)
+    values = values.astype(F32)
+    center = values - jnp.mean(values, axis=-1, keepdims=True)
     return center, lax.rsqrt(row_means((center * center).astype(BF16), ones) + 1e-05)
 
 
@@ -61,7 +62,7 @@
     lnb, wpbt, tokens, cot, lnt, wq, wk, wv, wg, wo,
     pair_out, tokens_out, bg,
     wt, w_op, xd, cd,
-    ones_ref, normed, made, lf, rf, lm, rslab, part, z_recv, y_recv, own_sum, x_send, x_recv, slab, q_s, kslab,
+    ones_ref, wp2, normed, made, lf, rf, lm, rslab, part, z_recv, y_recv, own_sum, x_send, x_recv, slab, q_s, kslab,
     vslab, gate_s, datt_s, tri_send, tri_recv, tri_f, hb_f, hb_send, hb, bias, raw, d_probs, acc, g_send, g_recv,
     pj_send, py_recv, px_own, px_send, px_recv, sg, cg, cg_f,
     slab_ss, slab_rs, ring_ss, ring_rs, z_ss, z_rs, y_ss, y_rs, x_ss, x_rs,
@@ -115,6 +116,13 @@
     for n, w in enumerate((w_ag, w_av, w_bg, w_bv)):
         wt[n] = w[...].astype(F32).T.astype(BF16)
     wp = jnp.concatenate([wt[n, pl.ds(pl.multiple_of(samp * 32, 32), 32), :] for n in range(4)], axis=0)
+    wp2[...] = jnp.concatenate(
+        [
+            jnp.concatenate([wp, jnp.zeros((128, 128), BF16)], axis=1),
+            jnp.concatenate([jnp.zeros((128, 128), BF16), wp], axis=1),
+        ],
+        axis=0,
+    )
     tri_f[0:128, :] = w_outproj[...].astype(F32)
     w_op[...] = jnp.concatenate(
         [tri_f[pl.ds(0, 64, stride=2), :], tri_f[pl.ds(1, 64, stride=2), :]], axis=0
@@ -140,8 +148,10 @@
         normed[dst, :] = (normalize(pair[src, :], ones) * lnp[...]).astype(BF16)
 
     def made_chunk(m):
-        at = pl.ds(pl.multiple_of(m * CR, CR), CR)
-        made[at, :] = nt(normed[at, :], wp)
+        halves = [pl.ds(pl.multiple_of(m * CR + n * (CR // 2), CR // 2), CR // 2) for n in range(2)]
+        o = nt(jnp.concatenate([normed[at, :] for at in halves], axis=1), wp2[...])
+        for n, at in enumerate(halves):
+            made[at, :] = o[:, n * 128 : n * 128 + 128]
 
     def edge(o, first, kept):
         return jax.nn.sigmoid(o[first : first + 32]) * o[first + 32 : first + 64] * kept
@@ -717,6 +727,7 @@
         vm((128, 128), BF16),
         vm((2 * B, NC * B), F32),
         vm((2 * B, NC * B), F32),
+        vm((256, 256), BF16),
         vm((256, 256), BF16),
         vm((6 * CR, 128), BF16),
         vm((B * B + 32, 128), F32),

time: 161 us -> 159 us (0.988)
  Pallas kernels: 160 us -> 158 us
    pallas_call x1, Pallas kernels: 10.4 us -> 8.78 us  [per_device(): pl.pallas_call(finish, grid=(B // 16,), out_shape=(jax.ShapeDtypeStruct((...]
where the time goes in v8:
time: 159 us; the launch traced here: 158 us
  Pallas kernels  158 us (99%)
    pallas_call x1, Pallas kernels, per_device(): pl.pallas_call(kernel, out_shape=(jax.ShapeDtypeStruct((B * B, 128), BF16...  149 us
    pallas_call x1, Pallas kernels, per_device(): pl.pallas_call(finish, grid=(B // 16,), out_shape=(jax.ShapeDtypeStruct((...  8.78 us

profile of v8, /device:TPU:1, one launch (start us, length us, event | category | flops | bytes accessed | tf_op | source)
XLA Modules:
  0.0 158.3 jit_solution(2694352756628594273)
XLA Ops:
  0.6 148.8 %shard_map.229 = (bf16[9216,128]{1,0:T(8,128)(2,1)}, bf16[384,96]{1,0:T(8,128)(2,1)}, bf16[4,24,16,128]{3,2,1,0:T(8,128)(2,1)}) custom-call(bf16[9216,128]{1,0:T(8,128)(2,1)} %bitcast.16, s32[768]{0:T(1024)} %crop_s.1, s32[6,128]{1,0:T(8,128)} %bitcast.26, bf16[128,128]{1,0:T(8,128)(2,1)} %w_ag.1, bf16[128,128]{1,0:T(8,128)(2,1)} %w_av.1, ...), custom_call_target="tpu_custom_call" | custom-call | tf_op jit(solution)/shard_map/pallas_call | solution.py:778
  149.5 8.8 %shard_map.230 = (bf16[9216,128]{1,0:T(8,128)(2,1)}, bf16[384,96]{1,0:T(8,128)(2,1)}, f32[9216,128]{1,0:T(8,128)}) custom-call(bf16[9216,128]{1,0:T(8,128)(2,1)} %get-tuple-element.9.pair_rows, bf16[384,96]{1,0:T(8,128)(2,1)} %get-tuple-element.10.token_rows, bf16[96,16,128]{2,1,0:T(8,128)(2,1)} %bitcast.17, f32[1,128]{1,0:T(1,128)} %bitcast.29, ...), custom_call_target="tpu_custom_call" | custom-call | tf_op jit(solution)/shard_map/pallas_call | solution.py:794

commit v9 on v8

--- a/solution.py
+++ b/solution.py
@@ -124,9 +124,12 @@
         axis=0,
     )
     tri_f[0:128, :] = w_outproj[...].astype(F32)
-    w_op[...] = jnp.concatenate(
+    w_op[0:128, 0:128] = jnp.concatenate(
         [tri_f[pl.ds(0, 64, stride=2), :], tri_f[pl.ds(1, 64, stride=2), :]], axis=0
     ).astype(BF16)
+    w_op[0:128, 128:256] = jnp.zeros((128, 128), BF16)
+    w_op[128:256, 0:128] = jnp.zeros((128, 128), BF16)
+    w_op[128:256, 128:256] = w_outgate[...]
     crop = jnp.concatenate([crop_v[i : i + 1, :] for i in range(6)], axis=1).astype(F32)
     token_gain = jnp.concatenate([lnt[i : i + 1, :] for i in range(6)], axis=1)
 
@@ -453,13 +456,13 @@
         t = jnp.concatenate(cols, axis=1)
         center = t - jnp.mean(t, axis=0, keepdims=True)
         t = center * lax.rsqrt(jnp.mean(center * center, axis=0, keepdims=True) + 1e-05)
-        proj = tn(t.astype(BF16), w_op[...])
-        proj = jnp.concatenate([proj[e * 128 : e * 128 + B] for e in range(4)], axis=0)
+        t = t.T.astype(BF16)
+        t = jnp.concatenate([t[e * 128 : e * 128 + B] for e in range(4)], axis=0)
         first = row0 + m * 4
         at = pl.ds(pl.multiple_of(first * B, 4 * B), 4 * B)
         norm_at = pl.ds(pl.multiple_of(first // 16 * CR + first % 16 * B, 32), 4 * B)
-        gate = jax.nn.sigmoid(nn(normed[norm_at, :], w_outgate[...]))
-        updated = (pair[at, :].astype(F32) + gate * proj).astype(BF16)
+        o = nn(jnp.concatenate([t, normed[norm_at, :]], axis=1), w_op[...])
+        updated = (pair[at, :].astype(F32) + jax.nn.sigmoid(o[:, 128:]) * o[:, :128]).astype(BF16)
         trans_in = normalize(updated, ones).astype(BF16)
         total = updated.astype(F32)
         for n in range(2):
@@ -703,7 +706,7 @@
         )
         center, inv = centered(pair_rows[at, :], ones)
         unit = center * inv
-        pair_grad[at, :] = inv * (scaled - unit * row_means((scaled * unit).astype(BF16), ones))
+        pair_grad[at, :] = inv * (scaled - unit * jnp.mean(scaled * unit, axis=-1, keepdims=True))
 
 
 def per_device(
@@ -724,7 +727,7 @@
     dma = pltpu.SemaphoreType.DMA
     scratch = [
         vm((4, 128, 128), BF16),
-        vm((128, 128), BF16),
+        vm((256, 256), BF16),
         vm((2 * B, NC * B), F32),
         vm((2 * B, NC * B), F32),
         vm((256, 256), BF16),

time: 159 us -> 158 us (level)
  no operation moved by 1% of the time
where the time goes in v9:
time: 158 us
  Pallas kernels  157 us (99%)
    pallas_call x1, Pallas kernels, per_device(): pl.pallas_call(kernel, out_shape=(jax.ShapeDtypeStruct((B * B, 128), BF16...  149 us
    pallas_call x1, Pallas kernels, per_device(): pl.pallas_call(finish, grid=(B // 16,), out_shape=(jax.ShapeDtypeStruct((...  8.49 us

profile of v9, /device:TPU:1, one launch (start us, length us, event | category | flops | bytes accessed | tf_op | source)
XLA Modules:
  0.0 158.0 jit_solution(9261351495043022981)
XLA Ops:
  0.6 148.9 %shard_map.229 = (bf16[9216,128]{1,0:T(8,128)(2,1)}, bf16[384,96]{1,0:T(8,128)(2,1)}, bf16[4,24,16,128]{3,2,1,0:T(8,128)(2,1)}) custom-call(bf16[9216,128]{1,0:T(8,128)(2,1)} %bitcast.16, s32[768]{0:T(1024)} %crop_s.1, s32[6,128]{1,0:T(8,128)} %bitcast.26, bf16[128,128]{1,0:T(8,128)(2,1)} %w_ag.1, bf16[128,128]{1,0:T(8,128)(2,1)} %w_av.1, ...), custom_call_target="tpu_custom_call" | custom-call | tf_op jit(solution)/shard_map/pallas_call | solution.py:781
  149.6 8.5 %shard_map.230 = (bf16[9216,128]{1,0:T(8,128)(2,1)}, bf16[384,96]{1,0:T(8,128)(2,1)}, f32[9216,128]{1,0:T(8,128)}) custom-call(bf16[9216,128]{1,0:T(8,128)(2,1)} %get-tuple-element.9.pair_rows, bf16[384,96]{1,0:T(8,128)(2,1)} %get-tuple-element.10.token_rows, bf16[96,16,128]{2,1,0:T(8,128)(2,1)} %bitcast.17, f32[1,128]{1,0:T(1,128)} %bitcast.29, ...), custom_call_target="tpu_custom_call" | custom-call | tf_op jit(solution)/shard_map/pallas_call | solution.py:797
